TPU v7x, 32 devices: a whole 2x2x4 slice. The times are simulated.
32 devices in a mesh: rows: 16 (over z, y, x), ch: 2 (over core).
Axes of the slice: x: 2, y: 2, z: 4, core: 2. Of those that a mesh axis runs over, the one named last changes fastest.
Arguments:
- tokens: bfloat16 [2, 16, 256, 768], P(None, 'rows', None, 'ch'), may hold values from -6 to 6
- heights: int32 [2], replicated, may hold values from 4 to 16, as said below
- widths: int32 [2], replicated, may hold values from 64 to 256, as said below
- log_step: float32 [2, 768], P(None, 'ch'), may hold values from -0.7 to 0.7
- log_decay: float32 [2, 768, 32], P(None, 'ch'), as said below
- frequency: float32 [2, 768, 32], P(None, 'ch'), may hold values from 0 to 1
- b_in: float32 [2, 2, 768, 32], P(None, None, 'ch'), may hold values from -6 to 6
- c_out: float32 [2, 2, 768, 32], P(None, None, 'ch'), may hold values from -0.0625 to 0.0625
- skip_gain: float32 [768], P('ch'), may hold values from -3 to 3
- ln_gain: float32 [768], P('ch'), may hold values from 0.5 to 1.5
- ln_bias: float32 [768], P('ch'), may hold values from -1.75 to 1.75
- w_up: bfloat16 [768, 3072], P(None, 'ch'), may hold values from -0.21875 to 0.21875
- b_up: float32 [3072], P('ch'), may hold values from -1.75 to 1.75
- w_down: bfloat16 [3072, 768], P('ch'), may hold values from -0.109375 to 0.109375
- b_down: float32 [768], P('ch'), may hold values from -1.75 to 1.75
- layer_scale: float32 [768], P('ch'), may hold values from 0.5 to 1.5
- cotangent: bfloat16 [2, 16, 256, 768], P(None, 'rows', None, 'ch'), may hold values from -6 to 6
Outputs:
- output: bfloat16 [2, 16, 256, 768], P(None, 'rows', None, 'ch')
- d_tokens: bfloat16 [2, 16, 256, 768], P(None, 'rows', None, 'ch')
- d_log_step: float32 [2, 768], P(None, 'ch')
- d_log_decay: float32 [2, 768, 32], P(None, 'ch')
- d_frequency: float32 [2, 768, 32], P(None, 'ch')
- d_b_in: float32 [2, 2, 768, 32], P(None, None, 'ch')
- d_c_out: float32 [2, 2, 768, 32], P(None, None, 'ch')
- d_skip_gain: float32 [768], P('ch')
- d_ln_gain: float32 [768], P('ch')
- d_ln_bias: float32 [768], P('ch')
- d_w_up: float32 [768, 3072], P(None, 'ch')
- d_b_up: float32 [3072], P('ch')
- d_w_down: float32 [3072, 768], P('ch')
- d_b_down: float32 [768], P('ch')
- d_layer_scale: float32 [768], P('ch')
Inputs may be any that keep to these rules, and one draw needn't show every extreme that they name: `heights`: one grid, drawn from the seed, has exactly 16 rows; every other grid has fewer. `widths`: one grid, drawn from the seed, has exactly 256 columns; every other grid has fewer. exp(log_decay) times the axis's length (16 for height, 256 for width) lies between 0.25 and 8.
All inputs are finite; a program needn't handle non-finite values.
Results may differ from a plain program's by a relative error of at most 0.0077.
Values may be sent and summed in bfloat16 or wider, within the bound.
A program may use at most 128 MiB of HBM per device.

v0:
```python
import jax
import jax.numpy as jnp
from jax import lax
from jax.sharding import PartitionSpec as P

PRECISE = lax.Precision.HIGHEST
EPSILON = 1e-06


def make_tables(length):
    freq_ids = jnp.arange(length + 1, dtype=jnp.int32)[:, None]
    places = jnp.arange(length, dtype=jnp.int32)[None, :]
    turns = freq_ids * places % (2 * length)
    angles = turns.astype(jnp.float32) * (jnp.pi / length)
    cosine = jnp.cos(angles)
    sine_t = jnp.sin(angles)
    weights = jnp.where((freq_ids == 0) | (freq_ids == length), 1.0, 2.0) / (2.0 * length)
    return (cosine, sine_t, cosine * weights, sine_t * weights)


def to_spectrum(values, tables, pattern):
    real_part = jnp.einsum(pattern, tables[0], values, precision=PRECISE)
    imag_part = -jnp.einsum(pattern, tables[1], values, precision=PRECISE)
    return (real_part, imag_part)


def from_spectrum(real_part, imag_part, tables, pattern):
    return jnp.einsum(pattern, tables[2], real_part, precision=PRECISE) - jnp.einsum(
        pattern, tables[3], imag_part, precision=PRECISE
    )


def kernel_spectrum(kernel, tables):
    real_part = jnp.dot(tables[0], kernel, precision=PRECISE)
    imag_part = -jnp.dot(tables[1], kernel, precision=PRECISE)
    return (real_part, imag_part)


def kernel_from_cross(cross_re, cross_im, tables):
    contract = (((0,), (0,)), ((), ()))
    return lax.dot_general(tables[2], cross_re, contract, precision=PRECISE) - lax.dot_general(
        tables[3], cross_im, contract, precision=PRECISE
    )


def make_kernel(params, length):
    log_step, log_decay, frequency, b_in, c_out = params
    step_size = jnp.exp(log_step)[:, None]
    decay_re = -jnp.exp(log_decay)
    step_re = step_size * decay_re
    step_im = step_size * frequency
    half_sin = jnp.sin(0.5 * step_im)
    num_re = jnp.expm1(step_re) * jnp.cos(step_im) - 2.0 * half_sin * half_sin
    num_im = jnp.exp(step_re) * jnp.sin(step_im)
    divisor = decay_re * decay_re + frequency * frequency
    zoh_re = (num_re * decay_re + num_im * frequency) / divisor
    zoh_im = (num_im * decay_re - num_re * frequency) / divisor
    prod_re = b_in[0] * c_out[0] - b_in[1] * c_out[1]
    prod_im = b_in[0] * c_out[1] + b_in[1] * c_out[0]
    coef_re = prod_re * zoh_re - prod_im * zoh_im
    coef_im = prod_re * zoh_im + prod_im * zoh_re
    places = jnp.arange(length, dtype=jnp.float32)[:, None, None]
    fading = jnp.exp(step_re[None] * places)
    turning = step_im[None] * places
    return 2.0 * jnp.sum(fading * (coef_re * jnp.cos(turning) - coef_im * jnp.sin(turning)), axis=2)


def shards(
    tokens,
    heights,
    widths,
    log_step,
    log_decay,
    frequency,
    b_in,
    c_out,
    skip_gain,
    ln_gain,
    ln_bias,
    w_up,
    b_up,
    w_down,
    b_down,
    layer_scale,
    cotangent,
):
    row_count = lax.axis_size("rows")
    row_rank = lax.axis_index("rows")
    grid_count, rows_here, columns, channels = tokens.shape
    all_channels = channels * lax.axis_size("ch")
    height = rows_here * row_count
    own_count = channels // row_count
    first_chan = row_rank * own_count
    pixels = grid_count * rows_here * columns
    token_f = tokens.astype(jnp.float32)
    width_tables = make_tables(columns)
    height_tables = make_tables(height)
    width_params = (log_step[1], log_decay[1], frequency[1], b_in[1], c_out[1])
    height_params = (
        lax.dynamic_slice_in_dim(log_step[0], first_chan, own_count, 0),
        lax.dynamic_slice_in_dim(log_decay[0], first_chan, own_count, 0),
        lax.dynamic_slice_in_dim(frequency[0], first_chan, own_count, 0),
        lax.dynamic_slice_in_dim(b_in[0], first_chan, own_count, 1),
        lax.dynamic_slice_in_dim(c_out[0], first_chan, own_count, 1),
    )
    k_width, width_pull = jax.vjp(lambda params: make_kernel(params, columns), width_params)
    k_height, height_pull = jax.vjp(lambda params: make_kernel(params, height), height_params)
    kw_re, kw_im = kernel_spectrum(k_width, width_tables)
    kh_re, kh_im = kernel_spectrum(k_height, height_tables)
    kh_re = kh_re[:, None, :]
    kh_im = kh_im[:, None, :]
    x_re, x_im = to_spectrum(token_f, width_tables, "fw,grwc->grfc")
    along_width = from_spectrum(
        x_re * kw_re - x_im * kw_im, x_re * kw_im + x_im * kw_re, width_tables, "fw,grfc->grwc"
    ).astype(jnp.bfloat16)
    p_re, p_im = to_spectrum(
        lax.all_to_all(along_width, "rows", split_axis=3, concat_axis=1, tiled=True).astype(
            jnp.float32
        ),
        height_tables,
        "fh,ghwc->gfwc",
    )
    mixed_cols = from_spectrum(
        p_re * kh_re - p_im * kh_im, p_re * kh_im + p_im * kh_re, height_tables, "fh,gfwc->ghwc"
    ).astype(jnp.bfloat16)
    back_rows = lax.all_to_all(mixed_cols, "rows", split_axis=1, concat_axis=3, tiled=True)
    mixed = back_rows.astype(jnp.float32) + skip_gain * token_f
    flat_mixed = mixed.reshape(pixels, channels)
    sum_one, sum_two = lax.psum(
        (jnp.sum(flat_mixed, axis=1), jnp.sum(flat_mixed * flat_mixed, axis=1)), "ch"
    )
    centre = sum_one / all_channels
    spread = sum_two / all_channels - centre * centre
    inv_std = lax.rsqrt(spread + EPSILON)[:, None]
    x_hat = (flat_mixed - centre[:, None]) * inv_std
    normed = (x_hat * ln_gain + ln_bias).astype(jnp.bfloat16)
    hidden = (
        jnp.dot(
            lax.all_gather(normed, "ch", axis=1, tiled=True),
            w_up,
            preferred_element_type=jnp.float32,
        )
        + b_up
    )
    active = jax.nn.gelu(hidden, approximate=False).astype(jnp.bfloat16)
    partials = jnp.dot(active, w_down, preferred_element_type=jnp.float32)
    branch = (
        lax.psum_scatter(
            partials.astype(jnp.bfloat16), "ch", scatter_dimension=1, tiled=True
        ).astype(jnp.float32)
        + b_down
    )
    row_ids = row_rank * rows_here + jnp.arange(rows_here, dtype=jnp.int32)
    col_ids = jnp.arange(columns, dtype=jnp.int32)
    inside = (row_ids[None, :, None] < heights[:, None, None]) & (
        col_ids[None, None, :] < widths[:, None, None]
    )
    inside = inside.astype(jnp.float32).reshape(pixels, 1)
    flat_tokens = token_f.reshape(pixels, channels)
    output = (
        (flat_tokens + inside * layer_scale * branch).astype(jnp.bfloat16).reshape(tokens.shape)
    )
    over_rows = (((0,), (0,)), ((), ()))
    over_cols = (((1,), (1,)), ((), ()))
    g_flat = cotangent.astype(jnp.float32).reshape(pixels, channels)
    g_masked = g_flat * inside
    g_branch = (g_masked * layer_scale).astype(jnp.bfloat16)
    d_layer_scale = jnp.sum(g_masked * branch, axis=0)
    d_b_down = jnp.sum(g_branch.astype(jnp.float32), axis=0)
    g_branch_all = lax.all_gather(g_branch, "ch", axis=1, tiled=True)
    d_w_down = lax.dot_general(active, g_branch_all, over_rows, preferred_element_type=jnp.float32)
    g_active = lax.dot_general(g_branch_all, w_down, over_cols, preferred_element_type=jnp.float32)
    gelu_pull = jax.vjp(lambda values: jax.nn.gelu(values, approximate=False), hidden)[1]
    g_hidden = gelu_pull(g_active)[0].astype(jnp.bfloat16)
    d_b_up = jnp.sum(g_hidden.astype(jnp.float32), axis=0)
    d_w_up = lax.dot_general(
        lax.all_gather(normed, "ch", axis=1, tiled=True),
        g_hidden,
        over_rows,
        preferred_element_type=jnp.float32,
    )
    g_terms = lax.dot_general(g_hidden, w_up, over_cols, preferred_element_type=jnp.float32)
    g_normed = lax.psum_scatter(g_terms, "ch", scatter_dimension=1, tiled=True)
    d_ln_gain = jnp.sum(g_normed * x_hat, axis=0)
    d_ln_bias = jnp.sum(g_normed, axis=0)
    g_hat = g_normed * ln_gain
    sum_grad, sum_cross = lax.psum((jnp.sum(g_hat, axis=1), jnp.sum(g_hat * x_hat, axis=1)), "ch")
    g_mixed = inv_std * (
        g_hat - sum_grad[:, None] / all_channels - x_hat * sum_cross[:, None] / all_channels
    )
    d_skip_gain = jnp.sum(g_mixed * flat_tokens, axis=0)
    g_spatial = g_mixed.astype(jnp.bfloat16).reshape(tokens.shape)
    pencil_grad, pencil_vals = (
        lax.all_to_all(g_spatial, "rows", split_axis=3, concat_axis=1, tiled=True),
        lax.all_to_all(along_width, "rows", split_axis=3, concat_axis=1, tiled=True),
    )
    gp_re, gp_im = to_spectrum(pencil_grad.astype(jnp.float32), height_tables, "fh,ghwc->gfwc")
    vp_re, vp_im = to_spectrum(pencil_vals.astype(jnp.float32), height_tables, "fh,ghwc->gfwc")
    g_pencil_along = from_spectrum(
        gp_re * kh_re + gp_im * kh_im, gp_im * kh_re - gp_re * kh_im, height_tables, "fh,gfwc->ghwc"
    ).astype(jnp.bfloat16)
    cross_re = jnp.sum(vp_re * gp_re + vp_im * gp_im, axis=(0, 2))
    cross_im = jnp.sum(vp_re * gp_im - vp_im * gp_re, axis=(0, 2))
    dk_height = kernel_from_cross(cross_re, cross_im, height_tables)
    g_along = lax.all_to_all(g_pencil_along, "rows", split_axis=1, concat_axis=3, tiled=True)
    ga_re, ga_im = to_spectrum(g_along.astype(jnp.float32), width_tables, "fw,grwc->grfc")
    g_conv = from_spectrum(
        ga_re * kw_re + ga_im * kw_im, ga_im * kw_re - ga_re * kw_im, width_tables, "fw,grfc->grwc"
    )
    wide_re = jnp.sum(x_re * ga_re + x_im * ga_im, axis=(0, 1))
    wide_im = jnp.sum(x_re * ga_im - x_im * ga_re, axis=(0, 1))
    dk_width = kernel_from_cross(wide_re, wide_im, width_tables)
    d_tokens = ((g_flat + g_mixed * skip_gain).reshape(tokens.shape) + g_conv).astype(jnp.bfloat16)
    width_grads = width_pull(dk_width)[0]
    height_grads = height_pull(dk_height)[0]

    def widen(piece_grad, dim_num):
        full_shape = list(piece_grad.shape)
        full_shape[dim_num] = channels
        return lax.dynamic_update_slice_in_dim(
            jnp.zeros(full_shape, jnp.float32), piece_grad, first_chan, dim_num
        )

    d_log_step = jnp.stack([widen(height_grads[0], 0), width_grads[0]])
    d_log_decay = jnp.stack([widen(height_grads[1], 0), width_grads[1]])
    d_frequency = jnp.stack([widen(height_grads[2], 0), width_grads[2]])
    d_b_in = jnp.stack([widen(height_grads[3], 1), width_grads[3]])
    d_c_out = jnp.stack([widen(height_grads[4], 1), width_grads[4]])
    totals = lax.psum(
        (
            d_log_step,
            d_log_decay,
            d_frequency,
            d_b_in,
            d_c_out,
            d_skip_gain,
            d_ln_gain,
            d_ln_bias,
            d_w_up,
            d_b_up,
            d_w_down,
            d_b_down,
            d_layer_scale,
        ),
        "rows",
    )
    return (output, d_tokens) + tuple(totals)


def solution(mesh):
    return jax.shard_map(
        shards,
        mesh=mesh,
        in_specs=(
            P(None, "rows", None, "ch"),
            P(),
            P(),
            P(None, "ch"),
            P(None, "ch", None),
            P(None, "ch", None),
            P(None, None, "ch", None),
            P(None, None, "ch", None),
            P("ch"),
            P("ch"),
            P("ch"),
            P(None, "ch"),
            P("ch"),
            P("ch", None),
            P("ch"),
            P("ch"),
            P(None, "rows", None, "ch"),
        ),
        out_specs=(
            P(None, "rows", None, "ch"),
            P(None, "rows", None, "ch"),
            P(None, "ch"),
            P(None, "ch", None),
            P(None, "ch", None),
            P(None, None, "ch", None),
            P(None, None, "ch", None),
            P("ch"),
            P("ch"),
            P("ch"),
            P(None, "ch"),
            P("ch"),
            P("ch", None),
            P("ch"),
            P("ch"),
        ),
        check_vma=False,
    )
```

profile of v0, /device:TPU:0, one launch (start us, length us, event | category | flops | bytes accessed | tf_op | source)
XLA Modules:
  0.0 624.9 jit_solution(703671772273096588)
XLA Ops:
  10.7 53.8 %multiply_reduce_fusion.4 = f32[256,384]{1,0:T(8,128)S(1)} fusion(f32[384,32]{0,1:T(8,128)S(1)} %add_bitcast_fusion.2, f32[384,32]{0,1:T(8,128)S(1)} %get-tuple-element.176, f32[384,32]{0,1:T(8,128)S(1)} %get-tuple-element.155, f32[384,32]{0,1:T(8,128)S(1)} %get-tuple-element.175), kind=kLoop, calls=%fused_computation.4 | loop fusion | flops 21921792 | bytes 589824 | tf_op jit(solution)/shard_map/jvp()/reduce_sum | solution.py:65
  74.0 3.3 fusion.18
  78.6 8.3 %all-to-all-start = ((bf16[2,1,256,384]{2,0,1,3:T(2,128)(2,1)}), bf16[2,1,256,384]{2,0,1,3:T(2,128)(2,1)S(1)}, u32[]{:S(2)}, u32[]{:S(2)}) async-start(bf16[2,1,256,384]{2,0,1,3:T(2,128)(2,1)} %copy.125), calls=%async_computation | async-start | bytes 786432 | tf_op jit(solution)/shard_map/all_to_all | solution.py:117
  91.2 8.3 %all-to-all-done = bf16[2,1,256,384]{2,0,1,3:T(2,128)(2,1)S(1)} async-done(((bf16[2,1,256,384]{2,0,1,3:T(2,128)(2,1)}), bf16[2,1,256,384]{2,0,1,3:T(2,128)(2,1)S(1)}, u32[]{:S(2)}, u32[]{:S(2)}) %all-to-all-start) | async-done | bytes 393248 | tf_op jit(solution)/shard_map/all_to_all | solution.py:117
  107.0 4.2 all-to-all-start.1
  119.3 3.4 all-to-all-done.1
  141.0 10.4 %convert_reduce_fusion = (f32[1536]{0:T(1024)}, bf16[512,1536]{1,0:T(8,128)(2,1)}, f32[512,1536]{1,0:T(8,128)S(1)}) fusion(f32[512,1536]{1,0:T(8,128)S(1)} %convolution_add_fusion, bf16[512,768]{1,0:T(8,128)(2,1)S(1)} %copy-done.18, bf16[1536,768]{1,0:T(8,128)(2,1)S(1)} %copy-done), kind=kOutput, calls=%fused_computation.15 | convolution fusion | flops 1266153984 | bytes 11016192 | tf_op jit(solution)/shard_map/dot_general | solution.py:172
  157.9 4.7 fusion.396
  166.7 10.8 %reduce-scatter.5.cloned.1.call-done = f32[512,384]{1,0:T(8,128)} async-done(((f32[512,768]{1,0:T(8,128)}), f32[512,384]{1,0:T(8,128)}) %reduce-scatter.5.cloned.1.call-update) | async-done | bytes 786448 | tf_op jit(solution)/shard_map/reduce_scatter | solution.py:183
  179.9 3.1 all-reduce.18
  183.8 3.8 fusion.71
  191.4 7.1 %all-to-all-start.2 = ((bf16[2,1,256,384]{2,0,1,3:T(2,128)(2,1)}), bf16[2,1,256,384]{2,0,1,3:T(2,128)(2,1)}, u32[]{:S(2)}, u32[]{:S(2)}) async-start(bf16[2,1,256,384]{2,0,1,3:T(2,128)(2,1)} %copy.137), calls=%async_computation.3 | async-start | bytes 786432 | tf_op jit(solution)/shard_map/all_to_all | solution.py:194
  198.5 5.4 fusion.397
  203.9 3.6 fusion.398
  207.5 4.0 all-to-all-done.2
  220.6 4.2 all-to-all-start.3
  229.1 7.3 %all-to-all-done.3 = bf16[2,16,256,24]{2,3,0,1:T(8,128)(2,1)} async-done(((bf16[2,16,256,24]{2,3,0,1:T(8,128)(2,1)}), bf16[2,16,256,24]{2,3,0,1:T(8,128)(2,1)}, u32[]{:S(2)}, u32[]{:S(2)}) %all-to-all-start.3) | async-done | bytes 393248 | tf_op jit(solution)/shard_map/all_to_all | solution.py:205
  239.0 4.1 fusion.51
  247.3 55.1 %multiply_reduce_fusion = (f32[384,32]{0,1:T(8,128)S(1)}, f32[384,32]{0,1:T(8,128)S(1)}, f32[384,32]{0,1:T(8,128)S(1)}, f32[384,32]{0,1:T(8,128)S(1)}) fusion(f32[256,384]{1,0:T(8,128)S(1)} %fusion.19, f32[384,32]{0,1:T(8,128)S(1)} %copy-done.80, f32[384,32]{0,1:T(8,128)S(1)} %copy-done.76, f32[384,32]{0,1:T(8,128)S(1)} %copy-done.72, f32[384,32]{0,1:T(8,128)S(1)} %copy-done.74), kind=kLoop, calls=%fused_computation | loop fusion | flops 72302592 | bytes 786432 | tf_op jit(solution)/shard_map/transpose(jvp())/reduce_sum | solution.py:63
  315.6 4.6 fusion.46
  320.4 4.5 fusion.12
  330.5 78.0 %all-reduce.16 = (f32[2,384]{1,0:T(2,128)}, f32[384]{0:T(512)}, f32[384]{0:T(512)}, f32[384]{0:T(512)}, f32[1536]{0:T(1024)}, /*index=5*/f32[384]{0:T(512)}, f32[384]{0:T(512)}) all-reduce(f32[2,384]{1,0:T(2,128)S(1)} %pad_maximum_fusion.4, f32[384]{0:T(512)S(1)} %copy-done.92, ...), channel_id=1, replica_groups=mesh['rows'=16,'ch'=2] {'rows'}, use_global_device_ids=true, to_apply=%region_28.29 | all-reduce | flops 4224 | bytes 33792 | tf_op jit(solution)/shard_map/psum | solution.py:229
  408.5 196.1 %all-reduce.22.cloned.1.call-done = (f32[2,384,32]{1,2,0:T(8,128)}, f32[2,384,32]{1,2,0:T(8,128)}, f32[2,2,384,32]{2,3,1,0:T(8,128)}, f32[2,2,384,32]{2,3,1,0:T(...) async-done(((f32[2,384,32]{1,2,0:T(8,128)}, f32[2,384,32]{1,2,0:T(8,128)}, f32[2,2,384,32]{2,3,1,0:T(8,128)}, f32[2,2,384,32]{2,3,1,0:T(8,128)}, f32[768,1536]{1,0:T(8,128)}, ...) | async-done | bytes 10027024 | tf_op jit(solution)/shard_map/psum | solution.py:229
  611.0 4.9 copy.212
  (332 shorter events, 116.0 us)
Async XLA Ops:
  7.2 133.8 %copy-start = (bf16[1536,768]{1,0:T(8,128)(2,1)S(1)}, bf16[1536,768]{1,0:T(8,128)(2,1)}, u32[]{:S(2)}) copy-start(bf16[1536,768]{1,0:T(8,128)(2,1)} %param.30) | copy-start | bytes 7077892
  7.2 66.8 %copy-start.69 = (f32[257]{0:T(512)}, f32[257]{0:T(512)S(1)}, u32[]{:S(2)}) copy-start(f32[257]{0:T(512)S(1)} %select_multiply_fusion) | copy-start | bytes 3088
  8.1 78.8 %copy-start.101 = (f32[1,384]{1,0:T(1,128)}, f32[1,384]{1,0:T(1,128)S(1)}, u32[]{:S(2)}) copy-start(f32[1,384]{1,0:T(1,128)S(1)} %get-tuple-element.204) | copy-start | bytes 4612
  10.1 54.4 %copy-start.71 = (f32[384,32]{0,1:T(8,128)}, f32[384,32]{0,1:T(8,128)S(1)}, u32[]{:S(2)}) copy-start(f32[384,32]{0,1:T(8,128)S(1)} %get-tuple-element.155) | copy-start | bytes 147460
  10.1 54.4 %copy-start.73 = (f32[384,32]{0,1:T(8,128)}, f32[384,32]{0,1:T(8,128)S(1)}, u32[]{:S(2)}) copy-start(f32[384,32]{0,1:T(8,128)S(1)} %get-tuple-element.175) | copy-start | bytes 147460
  10.7 57.2 %copy-start.35 = (bf16[2,1,256,384]{3,2,1,0:T(8,128)(2,1)S(1)}, bf16[2,1,256,384]{3,2,1,0:T(8,128)(2,1)}, u32[]{:S(2)}) copy-start(bf16[2,1,256,384]{3,2,1,0:T(8,128)(2,1)} %param.17) | copy-start | bytes 1179652
  78.6 21.0 %all-to-all-start = ((bf16[2,1,256,384]{2,0,1,3:T(2,128)(2,1)}), bf16[2,1,256,384]{2,0,1,3:T(2,128)(2,1)S(1)}, u32[]{:S(2)}, u32[]{:S(2)}) async-start(bf16[2,1,256,384]{2,0,1,3:T(2,128)(2,1)} %copy.125), calls=%async_computation | async-start | bytes 786432 | tf_op jit(solution)/shard_map/all_to_all | solution.py:117
  107.0 15.7 %all-to-all-start.1 = ((bf16[2,16,256,24]{2,3,0,1:T(8,128)(2,1)}), bf16[2,16,256,24]{2,3,0,1:T(8,128)(2,1)}, u32[]{:S(2)}, u32[]{:S(2)}) async-start(bf16[2,16,256,24]{2,3,0,1:T(8,128)(2,1)} %copy.134), calls=%async_computation.1 | async-start | bytes 786432 | tf_op jit(solution)/shard_map/all_to_all | solution.py:126
  111.2 53.6 %reduce-scatter.7.cloned.1.call-start = ((), (), s32[]{:S(2)}) async-start(), calls=%async_computation.7 | async-start | bytes 1179648
  157.9 19.6 %reduce-scatter.5.cloned.1.call-start = ((), (), s32[]{:S(2)}) async-start(), calls=%async_computation.6 | async-start | bytes 2359296 | tf_op jit(solution)/shard_map/reduce_scatter | solution.py:183
  191.4 20.1 %all-to-all-start.2 = ((bf16[2,1,256,384]{2,0,1,3:T(2,128)(2,1)}), bf16[2,1,256,384]{2,0,1,3:T(2,128)(2,1)}, u32[]{:S(2)}, u32[]{:S(2)}) async-start(bf16[2,1,256,384]{2,0,1,3:T(2,128)(2,1)} %copy.137), calls=%async_computation.3 | async-start | bytes 786432 | tf_op jit(solution)/shard_map/all_to_all | solution.py:194
  220.6 15.8 %all-to-all-start.3 = ((bf16[2,16,256,24]{2,3,0,1:T(8,128)(2,1)}), bf16[2,16,256,24]{2,3,0,1:T(8,128)(2,1)}, u32[]{:S(2)}, u32[]{:S(2)}) async-start(bf16[2,16,256,24]{2,3,0,1:T(8,128)(2,1)} %copy.140), calls=%async_computation.4 | async-start | bytes 786432 | tf_op jit(solution)/shard_map/all_to_all | solution.py:205
  224.9 379.7 %all-reduce.22.cloned.1.call-start = ((), (), s32[]{:S(2)}) async-start(), calls=%async_computation.8 | async-start | bytes 20054016 | tf_op jit(solution)/shard_map/psum | solution.py:229
  247.2 55.3 %copy-start.20 = (f32[2,384,32]{1,2,0:T(8,128)S(1)}, f32[2,384,32]{1,2,0:T(8,128)}, u32[]{:S(2)}) copy-start(f32[2,384,32]{1,2,0:T(8,128)} %param.22) | copy-start | bytes 294916
  247.2 55.3 %copy-start.21 = (f32[2,384,32]{1,2,0:T(8,128)S(1)}, f32[2,384,32]{1,2,0:T(8,128)}, u32[]{:S(2)}) copy-start(f32[2,384,32]{1,2,0:T(8,128)} %param.21) | copy-start | bytes 294916
  247.2 55.3 %copy-start.22 = (f32[2,2,384,32]{2,3,1,0:T(8,128)S(1)}, f32[2,2,384,32]{2,3,1,0:T(8,128)}, u32[]{:S(2)}) copy-start(f32[2,2,384,32]{2,3,1,0:T(8,128)} %param.23) | copy-start | bytes 589828
  247.2 55.2 %copy-start.26 = (f32[1,384,32]{1,2,0:T(8,128)S(1)}, f32[1,384,32]{1,2,0:T(8,128)}, u32[]{:S(2)}) copy-start(f32[1,384,32]{1,2,0:T(8,128)} %get-tuple-element.159) | copy-start | bytes 147460
  247.2 55.2 %copy-start.28 = (f32[1,384,32]{1,2,0:T(8,128)S(1)}, f32[1,384,32]{1,2,0:T(8,128)}, u32[]{:S(2)}) copy-start(f32[1,384,32]{1,2,0:T(8,128)} %copy-done.27) | copy-start | bytes 147460
  247.2 55.2 %copy-start.30 = (f32[1,384,32]{1,2,0:T(8,128)S(1)}, f32[1,384,32]{1,2,0:T(8,128)}, u32[]{:S(2)}) copy-start(f32[1,384,32]{1,2,0:T(8,128)} %copy-done.29) | copy-start | bytes 147460
  247.2 55.2 %copy-start.32 = (f32[1,384,32]{1,2,0:T(8,128)S(1)}, f32[1,384,32]{1,2,0:T(8,128)}, u32[]{:S(2)}) copy-start(f32[1,384,32]{1,2,0:T(8,128)} %copy-done.31) | copy-start | bytes 147460
  247.2 55.2 %copy-start.34 = (f32[1,384,32]{1,2,0:T(8,128)S(1)}, f32[1,384,32]{1,2,0:T(8,128)}, u32[]{:S(2)}) copy-start(f32[1,384,32]{1,2,0:T(8,128)} %copy-done.33) | copy-start | bytes 147460
  247.2 56.2 %copy-start.56 = (f32[1,384,32]{1,2,0:T(8,128)S(1)}, f32[1,384,32]{1,2,0:T(8,128)}, u32[]{:S(2)}) copy-start(f32[1,384,32]{1,2,0:T(8,128)} %copy-done.55) | copy-start | bytes 147460
  247.3 58.3 %copy-start.23 = (f32[2,2,384,32]{2,3,1,0:T(8,128)S(1)}, f32[2,2,384,32]{2,3,1,0:T(8,128)}, u32[]{:S(2)}) copy-start(f32[2,2,384,32]{2,3,1,0:T(8,128)} %param.24) | copy-start | bytes 589828
  247.3 58.3 %copy-start.37 = (f32[1,2,384,32]{2,3,1,0:T(8,128)S(1)}, f32[1,2,384,32]{2,3,1,0:T(8,128)}, u32[]{:S(2)}) copy-start(f32[1,2,384,32]{2,3,1,0:T(8,128)} %copy-done.36) | copy-start | bytes 294916
  (89 other events, 714.8 us)
Sparse Core Ops, SparseCore 0:
  158.0 6.2 reduce-scatter.6
  167.2 10.1 reduce-scatter.4
  307.2 297.2 all-reduce.21
where the time goes:
time: 630 us; the launch traced here: 625 us
  waiting for transfers between devices  230 us (37%)
  other arithmetic  145 us (23%)
  blocking collectives  89.2 us (14%)
  matrix products  74.7 us (12%)
  local copies, waits for them, and re-layouts  46.7 us (7%)
  starting transfers between devices  23.9 us (4%)
  between operations  15.7 us (2%)
    psum x1, waiting for transfers between devices, shards(): lax.psum((d_log_step, d_log_decay, d_frequency, d_b_in, d_c_out, d_skip_g...  196 us
    psum x1, blocking collectives, shards(): lax.psum((d_log_step, d_log_decay, d_frequency, d_b_in, d_c_out, d_skip_g...  78 us
    reduce_sum x2, other arithmetic, make_kernel(): fading = jnp.exp(step_re[None] * places)  56 us
    reduce_sum x2, other arithmetic, make_kernel(): jnp.sum(fading * (coef_re * jnp.cos(turning) - coef_im * jnp.sin(turning)...  54.6 us
    unnamed x226, local copies, waits for them, and re-layouts  28.1 us
  transfers between devices with their start and end apart: 7, of which 6 were waited for; matrix products, arithmetic and copies ran while one was open for 9% of the time, Pallas kernels for 0%

commit v1 on v0

--- a/solution.py
+++ b/solution.py
@@ -1,10 +1,15 @@
+import functools
+
 import jax
 import jax.numpy as jnp
 from jax import lax
+from jax.experimental import pallas as pl
+from jax.experimental.pallas import tpu as pltpu
 from jax.sharding import PartitionSpec as P
 
 PRECISE = lax.Precision.HIGHEST
 EPSILON = 1e-06
+MESH = pl.DeviceIdType.MESH
 
 
 def make_tables(length):
@@ -63,6 +68,220 @@
     fading = jnp.exp(step_re[None] * places)
     turning = step_im[None] * places
     return 2.0 * jnp.sum(fading * (coef_re * jnp.cos(turning) - coef_im * jnp.sin(turning)), axis=2)
+
+
+STAGES = 8
+
+
+def reduce_places():
+    rank, core = lax.axis_index("rows"), lax.axis_index("ch")
+    x, y, z = rank % 2, (rank // 2) % 2, rank // 4
+    near = z // 2
+    toward = 4 * (2 * near - 1)
+    middle = jnp.minimum(z * (3 - z), 1)
+    beside = (rank + 1 - 2 * x, core)
+    across = (rank + 2 - 4 * y, core)
+    return (
+        x,
+        y,
+        near,
+        middle,
+        beside,
+        across,
+        (rank - toward, core),
+        (rank + toward, core),
+    )
+
+
+def reduce_barrier(places):
+    middle = places[3]
+    barrier = pltpu.get_barrier_semaphore()
+    for target in places[4:7]:
+        pl.semaphore_signal(barrier, inc=1, device_id=target, device_id_type=MESH)
+
+    @pl.when(middle == 1)
+    def _():
+        pl.semaphore_signal(barrier, inc=1, device_id=places[7], device_id_type=MESH)
+
+    pl.semaphore_wait(barrier, 3 + middle)
+
+
+def reduce_stage(stage, c, role, places, keep, first, third, bufs):
+    near, inner, outer = places[2], places[6], places[7]
+    far = 1 - near
+    part, from_first, from_outer, from_inner, from_third, full, send, recv = bufs
+
+    def remote(src, dst, kind, target):
+        return pltpu.make_async_remote_copy(
+            src_ref=src,
+            dst_ref=dst,
+            send_sem=send.at[kind, c],
+            recv_sem=recv.at[kind, c],
+            device_id=target,
+            device_id_type=MESH,
+        )
+
+    def added(*refs):
+        total = refs[0][...].astype(jnp.float32)
+        for ref in refs[1:]:
+            total = total + ref[...].astype(jnp.float32)
+        return total.astype(jnp.bfloat16)
+
+    to_first = functools.partial(remote, part.at[c, 1 - keep], from_first.at[c], 0, first)
+    far_in = functools.partial(remote, part.at[c, keep, far], from_outer.at[c, 0], 1, inner)
+    near_in = functools.partial(remote, part.at[c, keep, near], from_outer.at[c, 1], 2, inner)
+    far_over = functools.partial(remote, part.at[c, keep, far], from_inner.at[c], 3, inner)
+    to_third = functools.partial(remote, part.at[c, keep, near], from_third.at[c], 4, third)
+    own_out = functools.partial(remote, full.at[c, keep, near], full.at[c, keep, near], 5, outer)
+    own_over = functools.partial(remote, full.at[c, keep, near], full.at[c, keep, near], 6, inner)
+    over_in = functools.partial(remote, full.at[c, keep, far], full.at[c, keep, far], 6, inner)
+    over_out = functools.partial(remote, full.at[c, keep, far], full.at[c, keep, far], 7, outer)
+    back = functools.partial(remote, full.at[c, keep], full.at[c, keep], 8, first)
+    back_in = functools.partial(remote, full.at[c, 1 - keep], full.at[c, 1 - keep], 8, first)
+    near_back = functools.partial(remote, full.at[c, keep, near], full.at[c, keep, near], 5, inner)
+    far_back = functools.partial(remote, full.at[c, keep, far], full.at[c, keep, far], 7, inner)
+    if stage == 0:
+
+        @pl.when(role > 0)
+        def _():
+            to_first().start()
+
+    elif stage == 1:
+
+        @pl.when(role > 0)
+        def _():
+            to_first().wait_recv()
+            part[c, keep] = added(part.at[c, keep], from_first.at[c])
+
+        @pl.when(role == 1)
+        def _():
+            far_in().start()
+            near_in().start()
+
+    elif stage == 2:
+
+        @pl.when(role == 2)
+        def _():
+            far_in().wait_recv()
+            part[c, keep, far] = added(part.at[c, keep, far], from_outer.at[c, 0])
+            far_over().start()
+
+    elif stage == 3:
+
+        @pl.when(role == 2)
+        def _():
+            near_in().wait_recv()
+            far_over().wait_recv()
+            part[c, keep, near] = added(
+                part.at[c, keep, near], from_outer.at[c, 1], from_inner.at[c]
+            )
+            to_third().start()
+
+    elif stage == 4:
+
+        @pl.when(role == 2)
+        def _():
+            to_third().wait_recv()
+            full[c, keep, near] = added(part.at[c, keep, near], from_third.at[c])
+            own_out().start()
+            own_over().start()
+
+    elif stage == 5:
+
+        @pl.when(role == 2)
+        def _():
+            over_in().wait_recv()
+            over_out().start()
+            back().start()
+
+    elif stage == 6:
+
+        @pl.when(role == 1)
+        def _():
+            near_back().wait_recv()
+            far_back().wait_recv()
+            back().start()
+
+    else:
+
+        @pl.when(role > 0)
+        def _():
+            back_in().wait_recv()
+            to_first().wait_send()
+            back().wait_send()
+
+        @pl.when(role == 2)
+        def _():
+            far_over().wait_send()
+            to_third().wait_send()
+            own_out().wait_send()
+            own_over().wait_send()
+            over_out().wait_send()
+
+        @pl.when(role == 1)
+        def _():
+            far_in().wait_send()
+            near_in().wait_send()
+
+
+def reduce_kernel(down_ref, up_ref, down_full, up_full, *scratch):
+    count = down_ref.shape[0]
+    places = reduce_places()
+    x, y, middle = places[0], places[1], places[3]
+    beside, across = places[4], places[5]
+    half = len(scratch) // 2
+    down = (down_ref,) + scratch[: half - 2] + (down_full,) + scratch[half - 2 : half]
+    up = (up_ref,) + scratch[half : 2 * half - 2] + (up_full,) + scratch[2 * half - 2 :]
+    reduce_barrier(places)
+
+    def tick(t, carry):
+        for stage in range(STAGES):
+            c = t - stage
+
+            live = (c * (count - 1 - c) >= 0).astype(jnp.int32)
+            role = live * (1 + middle)
+            reduce_stage(stage, c, role, places, x, beside, across, down)
+            reduce_stage(stage, c, role, places, y, across, beside, up)
+
+        return carry
+
+    lax.fori_loop(0, count + STAGES - 1, tick, 0)
+
+
+def reduce_scratch(shape):
+    count, _, _, rows, columns = shape
+    return [
+        pltpu.VMEM((count, 2, rows, columns), jnp.bfloat16),
+        pltpu.VMEM((count, 2, rows, columns), jnp.bfloat16),
+        pltpu.VMEM((count, rows, columns), jnp.bfloat16),
+        pltpu.VMEM((count, rows, columns), jnp.bfloat16),
+        pltpu.SemaphoreType.DMA((9, count)),
+        pltpu.SemaphoreType.DMA((9, count)),
+    ]
+
+
+def sum_weights(d_w_down, d_w_up, part):
+    hidden, channels = d_w_down.shape
+    count = hidden // part
+    down = d_w_down.astype(jnp.bfloat16).reshape(count, 2, 2, part // 4, channels)
+    up = d_w_up.astype(jnp.bfloat16).reshape(channels, count, part)
+    up = up.transpose(1, 0, 2).reshape(count, 2, 2, channels // 4, part)
+    in_vmem = pl.BlockSpec(memory_space=pltpu.VMEM)
+    down, up = pl.pallas_call(
+        reduce_kernel,
+        out_shape=(
+            jax.ShapeDtypeStruct(down.shape, down.dtype),
+            jax.ShapeDtypeStruct(up.shape, up.dtype),
+        ),
+        in_specs=[in_vmem] * 2,
+        out_specs=(in_vmem, in_vmem),
+        scratch_shapes=reduce_scratch(down.shape) + reduce_scratch(up.shape),
+        compiler_params=pltpu.CompilerParams(
+            collective_id=0, has_side_effects=True, vmem_limit_bytes=48 << 20
+        ),
+    )(down, up)
+    up = up.reshape(count, channels, part).transpose(1, 0, 2).reshape(channels, hidden)
+    return down.reshape(hidden, channels).astype(jnp.float32), up.astype(jnp.float32)
 
 
 def shards(
@@ -95,31 +314,30 @@
     token_f = tokens.astype(jnp.float32)
     width_tables = make_tables(columns)
     height_tables = make_tables(height)
-    width_params = (log_step[1], log_decay[1], frequency[1], b_in[1], c_out[1])
-    height_params = (
-        lax.dynamic_slice_in_dim(log_step[0], first_chan, own_count, 0),
-        lax.dynamic_slice_in_dim(log_decay[0], first_chan, own_count, 0),
-        lax.dynamic_slice_in_dim(frequency[0], first_chan, own_count, 0),
-        lax.dynamic_slice_in_dim(b_in[0], first_chan, own_count, 1),
-        lax.dynamic_slice_in_dim(c_out[0], first_chan, own_count, 1),
-    )
+    own_params = tuple(
+        lax.dynamic_slice_in_dim(param, first_chan, own_count, param.ndim - trailing)
+        for param, trailing in (
+            (log_step, 1),
+            (log_decay, 2),
+            (frequency, 2),
+            (b_in, 2),
+            (c_out, 2),
+        )
+    )
+    width_params = tuple(param[1] for param in own_params)
+    height_params = tuple(param[0] for param in own_params)
     k_width, width_pull = jax.vjp(lambda params: make_kernel(params, columns), width_params)
     k_height, height_pull = jax.vjp(lambda params: make_kernel(params, height), height_params)
     kw_re, kw_im = kernel_spectrum(k_width, width_tables)
     kh_re, kh_im = kernel_spectrum(k_height, height_tables)
     kh_re = kh_re[:, None, :]
     kh_im = kh_im[:, None, :]
-    x_re, x_im = to_spectrum(token_f, width_tables, "fw,grwc->grfc")
+    pencil_tokens = lax.all_to_all(tokens, "rows", split_axis=3, concat_axis=1, tiled=True)
+    x_re, x_im = to_spectrum(pencil_tokens.astype(jnp.float32), width_tables, "fw,grwc->grfc")
     along_width = from_spectrum(
         x_re * kw_re - x_im * kw_im, x_re * kw_im + x_im * kw_re, width_tables, "fw,grfc->grwc"
     ).astype(jnp.bfloat16)
-    p_re, p_im = to_spectrum(
-        lax.all_to_all(along_width, "rows", split_axis=3, concat_axis=1, tiled=True).astype(
-            jnp.float32
-        ),
-        height_tables,
-        "fh,ghwc->gfwc",
-    )
+    p_re, p_im = to_spectrum(along_width.astype(jnp.float32), height_tables, "fh,ghwc->gfwc")
     mixed_cols = from_spectrum(
         p_re * kh_re - p_im * kh_im, p_re * kh_im + p_im * kh_re, height_tables, "fh,gfwc->ghwc"
     ).astype(jnp.bfloat16)
@@ -190,23 +408,23 @@
     )
     d_skip_gain = jnp.sum(g_mixed * flat_tokens, axis=0)
     g_spatial = g_mixed.astype(jnp.bfloat16).reshape(tokens.shape)
-    pencil_grad, pencil_vals = (
-        lax.all_to_all(g_spatial, "rows", split_axis=3, concat_axis=1, tiled=True),
-        lax.all_to_all(along_width, "rows", split_axis=3, concat_axis=1, tiled=True),
-    )
+    pencil_grad = lax.all_to_all(g_spatial, "rows", split_axis=3, concat_axis=1, tiled=True)
     gp_re, gp_im = to_spectrum(pencil_grad.astype(jnp.float32), height_tables, "fh,ghwc->gfwc")
-    vp_re, vp_im = to_spectrum(pencil_vals.astype(jnp.float32), height_tables, "fh,ghwc->gfwc")
+    vp_re, vp_im = p_re, p_im
     g_pencil_along = from_spectrum(
         gp_re * kh_re + gp_im * kh_im, gp_im * kh_re - gp_re * kh_im, height_tables, "fh,gfwc->ghwc"
     ).astype(jnp.bfloat16)
     cross_re = jnp.sum(vp_re * gp_re + vp_im * gp_im, axis=(0, 2))
     cross_im = jnp.sum(vp_re * gp_im - vp_im * gp_re, axis=(0, 2))
     dk_height = kernel_from_cross(cross_re, cross_im, height_tables)
-    g_along = lax.all_to_all(g_pencil_along, "rows", split_axis=1, concat_axis=3, tiled=True)
+    g_along = g_pencil_along
     ga_re, ga_im = to_spectrum(g_along.astype(jnp.float32), width_tables, "fw,grwc->grfc")
     g_conv = from_spectrum(
         ga_re * kw_re + ga_im * kw_im, ga_im * kw_re - ga_re * kw_im, width_tables, "fw,grfc->grwc"
     )
+    g_conv = lax.all_to_all(
+        g_conv.astype(jnp.bfloat16), "rows", split_axis=1, concat_axis=3, tiled=True
+    ).astype(jnp.float32)
     wide_re = jnp.sum(x_re * ga_re + x_im * ga_im, axis=(0, 1))
     wide_im = jnp.sum(x_re * ga_im - x_im * ga_re, axis=(0, 1))
     dk_width = kernel_from_cross(wide_re, wide_im, width_tables)
@@ -214,37 +432,30 @@
     width_grads = width_pull(dk_width)[0]
     height_grads = height_pull(dk_height)[0]
 
-    def widen(piece_grad, dim_num):
-        full_shape = list(piece_grad.shape)
-        full_shape[dim_num] = channels
-        return lax.dynamic_update_slice_in_dim(
-            jnp.zeros(full_shape, jnp.float32), piece_grad, first_chan, dim_num
-        )
-
-    d_log_step = jnp.stack([widen(height_grads[0], 0), width_grads[0]])
-    d_log_decay = jnp.stack([widen(height_grads[1], 0), width_grads[1]])
-    d_frequency = jnp.stack([widen(height_grads[2], 0), width_grads[2]])
-    d_b_in = jnp.stack([widen(height_grads[3], 1), width_grads[3]])
-    d_c_out = jnp.stack([widen(height_grads[4], 1), width_grads[4]])
-    totals = lax.psum(
-        (
-            d_log_step,
-            d_log_decay,
-            d_frequency,
-            d_b_in,
-            d_c_out,
-            d_skip_gain,
-            d_ln_gain,
-            d_ln_bias,
-            d_w_up,
-            d_b_up,
-            d_w_down,
-            d_b_down,
-            d_layer_scale,
-        ),
-        "rows",
-    )
-    return (output, d_tokens) + tuple(totals)
+    def gathered(pieces, dim_num):
+        return lax.all_gather(jnp.stack(pieces), "rows", axis=dim_num, tiled=True)
+
+    param_grads = tuple(
+        gathered(pair, dim_num)
+        for pair, dim_num in zip(zip(height_grads, width_grads), (1, 1, 1, 2, 2))
+    )
+    if row_count == 16:
+        d_w_down, d_w_up = sum_weights(d_w_down, d_w_up, w_up.shape[1] // 12)
+    else:
+        d_w_down, d_w_up = lax.psum((d_w_down, d_w_up), "rows")
+    d_skip_gain, d_ln_gain, d_ln_bias, d_b_up, d_b_down, d_layer_scale = lax.psum(
+        (d_skip_gain, d_ln_gain, d_ln_bias, d_b_up, d_b_down, d_layer_scale), "rows"
+    )
+    return (output, d_tokens) + param_grads + (
+        d_skip_gain,
+        d_ln_gain,
+        d_ln_bias,
+        d_w_up,
+        d_b_up,
+        d_w_down,
+        d_b_down,
+        d_layer_scale,
+    )
 
 
 def solution(mesh):

time: 630 us -> 575 us (0.913)
  waiting for transfers between devices: 230 us -> 3.99 us
  blocking collectives: 89.2 us -> 289 us
  other arithmetic: 145 us -> 39.5 us
  Pallas kernels: 0 us -> 86.4 us
  matrix products: 74.7 us -> 60.7 us
    all_gather x0 -> x5, blocking collectives: none -> 201 us  [gathered(): return lax.all_gather(jnp.stack(pieces), 'rows', axis=dim_num, tiled=True)]
    psum x1 -> x0, waiting for transfers between devices: 196 us -> none  [shards(): lax.psum((d_log_step, d_log_decay, d_frequency, d_b_in, d_c_out, d_skip_g...]
    pallas_call x0 -> x1, Pallas kernels: none -> 86.4 us  [sum_weights(): pl.pallas_call(reduce_kernel, out_shape=(jax.ShapeDtypeStruct(down.shape,...]
    reduce_sum x2, other arithmetic: 56 us -> 5.6 us  [make_kernel(): fading = jnp.exp(step_re[None] * places)]
    reduce_sum x2, other arithmetic: 54.6 us -> 4.65 us  [make_kernel(): jnp.sum(fading * (coef_re * jnp.cos(turning) - coef_im * jnp.sin(turning)...]
    all_to_all x2, waiting for transfers between devices: 15.7 us -> 0.01 us  [the longest x1 0.01 us: shards(): lax.all_to_all(g_conv.astype(jnp.bfloat16), 'rows', split_axis=1, concat_...]
    reduce_scatter x1, waiting for transfers between devices: 10.8 us -> 0.01 us  [shards(): g_normed = lax.psum_scatter(g_terms, 'ch', scatter_dimension=1, tiled=True)]
    convert_element_type x2 -> x3, local copies, waits for them, and re-layouts: 2.01 us -> 10 us  [the longest x1 6.05 us: sum_weights(): up.astype(jnp.float32)]
  transfers between devices with their start and end apart: 7 -> 6, of which waited for: 6 -> 1; matrix products, arithmetic and copies ran while one was open for 9% -> 12% of each run, Pallas kernels for 0% -> 15%
where the time goes in v1:
time: 575 us; the launch traced here: 571 us
  blocking collectives  289 us (50%)
  Pallas kernels  86.4 us (15%)
  matrix products  60.7 us (11%)
  local copies, waits for them, and re-layouts  51.8 us (9%)
  other arithmetic  39.5 us (7%)
  starting transfers between devices  23 us (4%)
  between operations  16 us (3%)
    all_gather x5, blocking collectives, gathered(): return lax.all_gather(jnp.stack(pieces), 'rows', axis=dim_num, tiled=True)  201 us
    pallas_call x1, Pallas kernels, sum_weights(): pl.pallas_call(reduce_kernel, out_shape=(jax.ShapeDtypeStruct(down.shape,...  86.4 us
    psum x1, blocking collectives, shards(): lax.psum((d_skip_gain, d_ln_gain, d_ln_bias, d_b_up, d_b_down, d_layer_sc...  77.2 us
    unnamed x239, local copies, waits for them, and re-layouts  27.2 us
  transfers between devices with their start and end apart: 6, of which 1 were waited for; matrix products, arithmetic and copies ran while one was open for 12% of the time, Pallas kernels for 15%

profile of v1, /device:TPU:0, one launch (start us, length us, event | category | flops | bytes accessed | tf_op | source)
XLA Modules:
  0.0 570.8 jit_solution(10400297510356880336)
XLA Ops:
  9.3 8.3 %all-to-all-start = ((bf16[2,1,256,384]{2,0,1,3:T(2,128)(2,1)}), bf16[2,1,256,384]{2,0,1,3:T(2,128)(2,1)S(1)}, u32[]{:S(2)}, u32[]{:S(2)}) async-start(bf16[2,1,256,384]{2,0,1,3:T(2,128)(2,1)} %copy.212), calls=%async_computation | async-start | bytes 786432 | tf_op jit(solution)/shard_map/all_to_all | solution.py:335
  23.9 3.8 multiply_reduce_fusion.7
  45.6 6.9 %all-to-all-start.1 = ((bf16[2,16,256,24]{2,3,0,1:T(8,128)(2,1)}), bf16[2,16,256,24]{2,3,0,1:T(8,128)(2,1)}, u32[]{:S(2)}, u32[]{:S(2)}) async-start(bf16[2,16,256,24]{2,3,0,1:T(8,128)(2,1)} %copy.222), calls=%async_computation.1 | async-start | bytes 786432 | tf_op jit(solution)/shard_map/all_to_all | solution.py:344
  60.6 3.9 all-to-all-done.1
  71.2 3.1 all-reduce.18
  80.4 10.0 %convert_reduce_fusion = (f32[1536]{0:T(1024)}, bf16[512,1536]{1,0:T(8,128)(2,1)}, f32[512,1536]{1,0:T(8,128)S(1)}) fusion(f32[512,1536]{1,0:T(8,128)S(1)} %convolution_add_fusion, bf16[512,768]{1,0:T(8,128)(2,1)S(1)} %copy-done.14, bf16[1536,768]{1,0:T(8,128)(2,1)S(1)} %copy-done), kind=kOutput, calls=%fused_computation.5 | convolution fusion | flops 1266153984 | bytes 11016192 | tf_op jit(solution)/shard_map/dot_general | solution.py:390
  97.1 4.0 fusion.382
  105.3 4.2 convolution_convert_fusion
  109.5 3.2 copy.238
  115.1 4.5 convolution_convert_fusion.1
  119.7 86.4 %shard_map.280 = (bf16[12,2,2,32,768]{4,3,2,1,0:T(8,128)(2,1)S(1)}, bf16[12,2,2,192,128]{4,3,2,1,0:T(8,128)(2,1)S(1)}) custom-call(bf16[12,2,2,32,768]{4,3,2,1,0:T(8,128)(2,1)} %bitcast.673, bf16[12,2,2,192,128]{4,3,2,1,0:T(8,128)(2,1)} %bitcast.669), custom_call_target="tpu_custom_call" | custom-call | tf_op jit(solution)/shard_map/pallas_call | solution.py:270
  215.7 3.8 fusion.64
  222.7 4.2 all-to-all-start.2
  226.9 4.3 bitcast_convert_fusion.1
  231.2 6.1 %copy.240 = f32[12,768,128]{1,2,0:T(8,128)} copy(f32[12,768,128]{2,1,0:T(8,128)} %bitcast_convert_fusion.1) | data formatting | bytes 9437184 | tf_op jit(solution)/shard_map/convert_element_type | solution.py:284
  237.2 6.0 %copy.247 = f32[768,1536]{1,0:T(8,128)} copy(f32[768,1536]{0,1:T(8,128)} %bitcast.668) | data formatting | bytes 9437184
  248.4 77.2 %all-reduce.16 = (f32[384]{0:T(512)}, f32[384]{0:T(512)}, f32[384]{0:T(512)}, f32[1536]{0:T(1024)}, f32[384]{0:T(512)}, /*index=5*/f32[384]{0:T(512)}) all-reduce(f32[384]{0:T(512)S(1)} %copy-done.93, f32[384]{0:T(512)S(1)} %copy-done.96, f32[384]{0:T(512)S(1)} %copy-done.97, ...), channel_id=1, replica_groups=mesh['rows'=16,'ch'=2] {'rows'}, use_global_device_ids=true, to_apply=%region_29.30 | all-reduce | flops 3456 | bytes 27648 | tf_op jit(solution)/shard_map/psum | solution.py:446
  340.0 4.7 multiply_reduce_fusion.1
  350.8 3.6 all-to-all-start.3
  356.1 41.0 %all-gather = f32[16,24,2]{1,2,0:T(2,128)S(1)} all-gather(f32[1,24,2]{1,2,0:T(2,128)S(1)} %maximum_bitcast_fusion), channel_id=1, replica_groups=mesh['rows'=16,'ch'=2] {'rows'}, dimensions={0}, use_global_device_ids=true | all-gather | bytes 3264 | tf_op jit(solution)/shard_map/all_gather | solution.py:436
  397.9 37.8 %all_gather.26 = f32[2,384,32]{2,0,1:T(2,128)S(1)} all-gather(f32[2,24,32]{2,0,1:T(2,128)S(1)} %copy.235), channel_id=1, replica_groups=mesh['rows'=16,'ch'=2] {'rows'}, dimensions={1}, use_global_device_ids=true | all-gather | bytes 104448 | tf_op jit(solution)/shard_map/all_gather | solution.py:436
  436.5 40.1 %all_gather.25 = f32[2,384,32]{2,0,1:T(2,128)S(1)} all-gather(f32[2,24,32]{2,0,1:T(2,128)S(1)} %copy.234), channel_id=1, replica_groups=mesh['rows'=16,'ch'=2] {'rows'}, dimensions={1}, use_global_device_ids=true | all-gather | bytes 104448 | tf_op jit(solution)/shard_map/all_gather | solution.py:436
  477.3 40.6 %all_gather.27 = f32[2,2,384,32]{3,1,0,2:T(2,128)S(1)} all-gather(f32[2,2,24,32]{3,1,0,2:T(2,128)S(1)} %copy.236), channel_id=1, replica_groups=mesh['rows'=16,'ch'=2] {'rows'}, dimensions={2}, use_global_device_ids=true | all-gather | bytes 208896 | tf_op jit(solution)/shard_map/all_gather | solution.py:436
  519.1 41.7 %all_gather.28 = f32[2,2,384,32]{3,1,0,2:T(2,128)S(1)} all-gather(f32[2,2,24,32]{3,1,0,2:T(2,128)S(1)} %copy.237), channel_id=1, replica_groups=mesh['rows'=16,'ch'=2] {'rows'}, dimensions={2}, use_global_device_ids=true | all-gather | bytes 208896 | tf_op jit(solution)/shard_map/all_gather | solution.py:436
  (338 shorter events, 105.4 us)
Async XLA Ops:
  7.2 73.2 %copy-start = (bf16[1536,768]{1,0:T(8,128)(2,1)S(1)}, bf16[1536,768]{1,0:T(8,128)(2,1)}, u32[]{:S(2)}) copy-start(bf16[1536,768]{1,0:T(8,128)(2,1)} %param.30) | copy-start | bytes 7077892
  9.3 22.7 %all-to-all-start = ((bf16[2,1,256,384]{2,0,1,3:T(2,128)(2,1)}), bf16[2,1,256,384]{2,0,1,3:T(2,128)(2,1)S(1)}, u32[]{:S(2)}, u32[]{:S(2)}) async-start(bf16[2,1,256,384]{2,0,1,3:T(2,128)(2,1)} %copy.212), calls=%async_computation | async-start | bytes 786432 | tf_op jit(solution)/shard_map/all_to_all | solution.py:335
  18.4 12.1 %copy-start.79 = (f32[24]{0:T(128)}, f32[24]{0:T(128)S(1)}, u32[]{:S(2)}) copy-start(f32[24]{0:T(128)S(1)} %get-tuple-element.220) | copy-start | bytes 292
  18.4 12.1 %copy-start.81 = (f32[24]{0:T(128)}, f32[24]{0:T(128)S(1)}, u32[]{:S(2)}) copy-start(f32[24]{0:T(128)S(1)} %get-tuple-element.219) | copy-start | bytes 292
  19.4 8.9 %copy-start.23 = (f32[1,24,32]{2,1,0:T(8,128)}, f32[1,24,32]{2,1,0:T(8,128)S(1)}, u32[]{:S(2)}) copy-start(f32[1,24,32]{2,1,0:T(8,128)S(1)} %copy.276) | copy-start | bytes 9220
  19.6 8.7 %copy-start.21 = (f32[1,24,32]{2,1,0:T(8,128)}, f32[1,24,32]{2,1,0:T(8,128)S(1)}, u32[]{:S(2)}) copy-start(f32[1,24,32]{2,1,0:T(8,128)S(1)} %copy.262) | copy-start | bytes 9220
  19.6 8.7 %copy-start.25 = (f32[1,24,32]{2,1,0:T(8,128)}, f32[1,24,32]{2,1,0:T(8,128)S(1)}, u32[]{:S(2)}) copy-start(f32[1,24,32]{2,1,0:T(8,128)S(1)} %copy.271) | copy-start | bytes 9220
  20.7 11.2 %copy-start.41 = (f32[1,1,24,32]{3,2,1,0:T(8,128)}, f32[1,1,24,32]{3,2,1,0:T(8,128)S(1)}, u32[]{:S(2)}) copy-start(f32[1,1,24,32]{3,2,1,0:T(8,128)S(1)} %copy.272) | copy-start | bytes 9220
  20.8 11.1 %copy-start.38 = (f32[1,1,24,32]{3,2,1,0:T(8,128)}, f32[1,1,24,32]{3,2,1,0:T(8,128)S(1)}, u32[]{:S(2)}) copy-start(f32[1,1,24,32]{3,2,1,0:T(8,128)S(1)} %copy.267) | copy-start | bytes 9220
  20.9 11.0 %copy-start.50 = (f32[1,1,24,32]{3,2,1,0:T(8,128)}, f32[1,1,24,32]{3,2,1,0:T(8,128)S(1)}, u32[]{:S(2)}) copy-start(f32[1,1,24,32]{3,2,1,0:T(8,128)S(1)} %copy.274) | copy-start | bytes 9220
  21.0 10.9 %copy-start.44 = (f32[1,1,24,32]{3,2,1,0:T(8,128)}, f32[1,1,24,32]{3,2,1,0:T(8,128)S(1)}, u32[]{:S(2)}) copy-start(f32[1,1,24,32]{3,2,1,0:T(8,128)S(1)} %copy.275) | copy-start | bytes 9220
  21.2 10.7 %copy-start.47 = (f32[1,1,24,32]{3,2,1,0:T(8,128)}, f32[1,1,24,32]{3,2,1,0:T(8,128)S(1)}, u32[]{:S(2)}) copy-start(f32[1,1,24,32]{3,2,1,0:T(8,128)S(1)} %copy.273) | copy-start | bytes 9220
  21.5 10.5 %copy-start.67 = (f32[24,32]{1,0:T(8,128)}, f32[24,32]{1,0:T(8,128)S(1)}, u32[]{:S(2)}) copy-start(f32[24,32]{1,0:T(8,128)S(1)} %get-tuple-element.161) | copy-start | bytes 9220
  21.6 10.3 %copy-start.69 = (f32[24,32]{1,0:T(8,128)}, f32[24,32]{1,0:T(8,128)S(1)}, u32[]{:S(2)}) copy-start(f32[24,32]{1,0:T(8,128)S(1)} %get-tuple-element.197) | copy-start | bytes 9220
  21.7 10.3 %copy-start.71 = (f32[24,32]{1,0:T(8,128)}, f32[24,32]{1,0:T(8,128)S(1)}, u32[]{:S(2)}) copy-start(f32[24,32]{1,0:T(8,128)S(1)} %get-tuple-element.198) | copy-start | bytes 9220
  21.7 10.3 %copy-start.73 = (f32[24,32]{1,0:T(8,128)}, f32[24,32]{1,0:T(8,128)S(1)}, u32[]{:S(2)}) copy-start(f32[24,32]{1,0:T(8,128)S(1)} %get-tuple-element.199) | copy-start | bytes 9220
  23.6 8.3 %copy-start.55 = (f32[1,24,32]{2,1,0:T(8,128)}, f32[1,24,32]{2,1,0:T(8,128)S(1)}, u32[]{:S(2)}) copy-start(f32[1,24,32]{2,1,0:T(8,128)S(1)} %get-tuple-element.165) | copy-start | bytes 9220
  45.6 19.0 %all-to-all-start.1 = ((bf16[2,16,256,24]{2,3,0,1:T(8,128)(2,1)}), bf16[2,16,256,24]{2,3,0,1:T(8,128)(2,1)}, u32[]{:S(2)}, u32[]{:S(2)}) async-start(bf16[2,16,256,24]{2,3,0,1:T(8,128)(2,1)} %copy.222), calls=%async_computation.1 | async-start | bytes 786432 | tf_op jit(solution)/shard_map/all_to_all | solution.py:344
  52.5 155.0 %reduce-scatter.7.cloned.1.call-start = ((), (), s32[]{:S(2)}) async-start(), calls=%async_computation.7 | async-start | bytes 1179648
  97.0 112.4 %reduce-scatter.5.cloned.1.call-start = ((), (), s32[]{:S(2)}) async-start(), calls=%async_computation.6 | async-start | bytes 2359296 | tf_op jit(solution)/shard_map/reduce_scatter | solution.py:401
  222.7 103.0 %all-to-all-start.2 = ((bf16[2,1,256,384]{2,0,1,3:T(2,128)(2,1)}), bf16[2,1,256,384]{2,0,1,3:T(2,128)(2,1)}, u32[]{:S(2)}, u32[]{:S(2)}) async-start(bf16[2,1,256,384]{2,0,1,3:T(2,128)(2,1)} %copy.225), calls=%async_computation.3 | async-start | bytes 786432 | tf_op jit(solution)/shard_map/all_to_all | solution.py:411
  246.0 81.4 %copy-start.4 = (f32[2,17,256,24]{2,1,3,0:T(8,128)S(1)}, f32[2,17,256,24]{2,1,3,0:T(8,128)}, u32[]{:S(2)}) copy-start(f32[2,17,256,24]{2,1,3,0:T(8,128)} %copy-done.3) | copy-start | bytes 2506756
  350.8 211.2 %all-to-all-start.3 = ((bf16[2,16,256,24]{2,3,0,1:T(8,128)(2,1)}), bf16[2,16,256,24]{2,3,0,1:T(8,128)(2,1)S(1)}, u32[]{:S(2)}, u32[]{:S(2)}) async-start(bf16[2,16,256,24]{2,3,0,1:T(8,128)(2,1)} %copy.230), calls=%async_computation.4 | async-start | bytes 786432 | tf_op jit(solution)/shard_map/all_to_all | solution.py:425
  519.1 42.9 %copy-start.12 = (f32[2,1,256,384]{2,3,0,1:T(8,128)S(1)}, f32[2,1,256,384]{2,3,0,1:T(8,128)}, u32[]{:S(2)}) copy-start(f32[2,1,256,384]{2,3,0,1:T(8,128)} %copy.232) | copy-start | bytes 2359300
  (89 other events, 346.5 us)
Sparse Core Ops, SparseCore 0:
  97.1 6.2 reduce-scatter.6
  105.8 10.2 reduce-scatter.4

commit v2 on v1

--- a/solution.py
+++ b/solution.py
@@ -1,7 +1,9 @@
 import functools
+import types
 
 import jax
 import jax.numpy as jnp
+import numpy as np
 from jax import lax
 from jax.experimental import pallas as pl
 from jax.experimental.pallas import tpu as pltpu
@@ -70,44 +72,34 @@
     return 2.0 * jnp.sum(fading * (coef_re * jnp.cos(turning) - coef_im * jnp.sin(turning)), axis=2)
 
 
+RANKS = 16
 STAGES = 8
-
-
-def reduce_places():
-    rank, core = lax.axis_index("rows"), lax.axis_index("ch")
-    x, y, z = rank % 2, (rank // 2) % 2, rank // 4
-    near = z // 2
-    toward = 4 * (2 * near - 1)
-    middle = jnp.minimum(z * (3 - z), 1)
-    beside = (rank + 1 - 2 * x, core)
-    across = (rank + 2 - 4 * y, core)
-    return (
-        x,
-        y,
-        near,
-        middle,
-        beside,
-        across,
-        (rank - toward, core),
-        (rank + toward, core),
-    )
-
-
-def reduce_barrier(places):
-    middle = places[3]
-    barrier = pltpu.get_barrier_semaphore()
-    for target in places[4:7]:
-        pl.semaphore_signal(barrier, inc=1, device_id=target, device_id_type=MESH)
-
-    @pl.when(middle == 1)
-    def _():
-        pl.semaphore_signal(barrier, inc=1, device_id=places[7], device_id_type=MESH)
-
-    pl.semaphore_wait(barrier, 3 + middle)
+HIGH = lax.Precision.HIGH
+BF16 = jnp.bfloat16
+F32 = jnp.float32
+NT = (((1,), (1,)), ((), ()))
+TN = (((0,), (0,)), ((), ()))
+
+
+def spectral_tables(length):
+    turns = np.outer(np.arange(length), np.arange(length)) % (2 * length)
+    cosine = np.cos(np.pi * turns / length)
+    sine = np.sin(np.pi * turns / length)
+    sign = np.where(np.arange(length) % 2, -1.0, 1.0)
+    to_re, to_im = cosine.copy(), -sine
+    to_im[:, 0] = sign
+    from_re, from_im = cosine / length, -sine / length
+    from_re[0] /= 2
+    from_im[0] = sign / (2 * length)
+    return tuple(t.astype(np.float32) for t in (to_re, to_im, from_re, from_im))
+
+
+def times(a, b):
+    return a[0] * b[0] - a[1] * b[1], a[0] * b[1] + a[1] * b[0]
 
 
 def reduce_stage(stage, c, role, places, keep, first, third, bufs):
-    near, inner, outer = places[2], places[6], places[7]
+    near, inner, outer = places
     far = 1 - near
     part, from_first, from_outer, from_inner, from_third, full, send, recv = bufs
 
@@ -121,25 +113,34 @@
             device_id_type=MESH,
         )
 
+    def piece(which, kind, target):
+        place = full.at[c, keep, which]
+        return remote(place, place, kind, target)
+
     def added(*refs):
-        total = refs[0][...].astype(jnp.float32)
+        total = refs[0][...].astype(F32)
         for ref in refs[1:]:
-            total = total + ref[...].astype(jnp.float32)
-        return total.astype(jnp.bfloat16)
-
-    to_first = functools.partial(remote, part.at[c, 1 - keep], from_first.at[c], 0, first)
-    far_in = functools.partial(remote, part.at[c, keep, far], from_outer.at[c, 0], 1, inner)
-    near_in = functools.partial(remote, part.at[c, keep, near], from_outer.at[c, 1], 2, inner)
-    far_over = functools.partial(remote, part.at[c, keep, far], from_inner.at[c], 3, inner)
-    to_third = functools.partial(remote, part.at[c, keep, near], from_third.at[c], 4, third)
-    own_out = functools.partial(remote, full.at[c, keep, near], full.at[c, keep, near], 5, outer)
-    own_over = functools.partial(remote, full.at[c, keep, near], full.at[c, keep, near], 6, inner)
-    over_in = functools.partial(remote, full.at[c, keep, far], full.at[c, keep, far], 6, inner)
-    over_out = functools.partial(remote, full.at[c, keep, far], full.at[c, keep, far], 7, outer)
-    back = functools.partial(remote, full.at[c, keep], full.at[c, keep], 8, first)
-    back_in = functools.partial(remote, full.at[c, 1 - keep], full.at[c, 1 - keep], 8, first)
-    near_back = functools.partial(remote, full.at[c, keep, near], full.at[c, keep, near], 5, inner)
-    far_back = functools.partial(remote, full.at[c, keep, far], full.at[c, keep, far], 7, inner)
+            total = total + ref[...].astype(F32)
+        return total.astype(BF16)
+
+    def to_first():
+        return remote(part.at[c, 1 - keep], from_first.at[c], 0, first)
+
+    def far_in():
+        return remote(part.at[c, keep, far], from_outer.at[c, 0], 1, inner)
+
+    def near_in():
+        return remote(part.at[c, keep, near], from_outer.at[c, 1], 2, inner)
+
+    def far_over():
+        return remote(part.at[c, keep, far], from_inner.at[c], 3, inner)
+
+    def to_third():
+        return remote(part.at[c, keep, near], from_third.at[c], 4, third)
+
+    def back(half):
+        return remote(full.at[c, half], full.at[c, half], 8, first)
+
     if stage == 0:
 
         @pl.when(role > 0)
@@ -183,40 +184,40 @@
         def _():
             to_third().wait_recv()
             full[c, keep, near] = added(part.at[c, keep, near], from_third.at[c])
-            own_out().start()
-            own_over().start()
+            piece(near, 5, outer).start()
+            piece(near, 6, inner).start()
 
     elif stage == 5:
 
         @pl.when(role == 2)
         def _():
-            over_in().wait_recv()
-            over_out().start()
-            back().start()
+            piece(far, 6, inner).wait_recv()
+            piece(far, 7, outer).start()
+            back(keep).start()
 
     elif stage == 6:
 
         @pl.when(role == 1)
         def _():
-            near_back().wait_recv()
-            far_back().wait_recv()
-            back().start()
+            piece(near, 5, inner).wait_recv()
+            piece(far, 7, inner).wait_recv()
+            back(keep).start()
 
     else:
 
         @pl.when(role > 0)
         def _():
-            back_in().wait_recv()
+            back(1 - keep).wait_recv()
             to_first().wait_send()
-            back().wait_send()
+            back(keep).wait_send()
 
         @pl.when(role == 2)
         def _():
             far_over().wait_send()
             to_third().wait_send()
-            own_out().wait_send()
-            own_over().wait_send()
-            over_out().wait_send()
+            piece(near, 5, outer).wait_send()
+            piece(near, 6, inner).wait_send()
+            piece(far, 7, outer).wait_send()
 
         @pl.when(role == 1)
         def _():
@@ -224,64 +225,945 @@
             near_in().wait_send()
 
 
-def reduce_kernel(down_ref, up_ref, down_full, up_full, *scratch):
-    count = down_ref.shape[0]
-    places = reduce_places()
-    x, y, middle = places[0], places[1], places[3]
-    beside, across = places[4], places[5]
-    half = len(scratch) // 2
-    down = (down_ref,) + scratch[: half - 2] + (down_full,) + scratch[half - 2 : half]
-    up = (up_ref,) + scratch[half : 2 * half - 2] + (up_full,) + scratch[2 * half - 2 :]
-    reduce_barrier(places)
+def mode_values(modes):
+    log_step, log_decay, freq, b_re, b_im, c_re, c_im = (modes[2 * q : 2 * q + 2] for q in range(7))
+    step = jnp.exp(log_step)
+    decay = -jnp.exp(log_decay)
+    step_re = step * decay
+    step_im = step * freq
+    half_sin = jnp.sin(0.5 * step_im)
+    series = jnp.ones_like(step_re)
+    for order in range(11, 1, -1):
+        series = 1.0 + series * step_re * (1.0 / order)
+    grown = jnp.exp(step_re)
+    less_one = jnp.where(step_re > -0.5, step_re * series, grown - 1.0)
+    num_re = less_one * jnp.cos(step_im) - 2.0 * half_sin * half_sin
+    num_im = grown * jnp.sin(step_im)
+    inverse = 1.0 / (decay * decay + freq * freq)
+    over = (decay * inverse, -freq * inverse)
+    zoh = times((num_re, num_im), over)
+    b, c = (b_re, b_im), (c_re, c_im)
+    prod = times(b, c)
+    return types.SimpleNamespace(
+        step=step,
+        rate=(decay, freq),
+        over=over,
+        step_re=step_re,
+        step_im=step_im,
+        once=(num_re + 1.0, num_im),
+        zoh=zoh,
+        b=b,
+        c=c,
+        prod=prod,
+        coef=times(prod, zoh),
+    )
+
+
+def block_kernel(names, *refs):
+    v = types.SimpleNamespace(**dict(zip(names, refs)))
+    rank, core = lax.axis_index("rows"), lax.axis_index("ch")
+    x, y, z = rank % 2, (rank // 2) % 2, rank // 4
+    near = z // 2
+    toward = 4 * (2 * near - 1)
+    middle = jnp.minimum(z * (3 - z), 1)
+    beside, across = (rank + 1 - 2 * x, core), (rank + 2 - 4 * y, core)
+    places = (near, (rank - toward, core), (rank + toward, core))
+    twin = (rank, 1 - core)
+    heights, widths = v.heights, v.widths
+    chunks, part = v.wd.shape[0], v.wd.shape[1]
+    slab, columns = v.rb1.shape[1:]
+    own = slab // 2
+    here = own * RANKS
+    pixels = 2 * columns
+    per = v.log_decay.shape[1]
+    lanes = own * per
+
+    def copy(src, dst, sems, index, target):
+        return pltpu.make_async_remote_copy(
+            src_ref=src,
+            dst_ref=dst,
+            send_sem=sems.at[0, index],
+            recv_sem=sems.at[1, index],
+            device_id=target,
+            device_id_type=MESH,
+        )
+
+    def loop(count, body, start=0):
+        def step(i, carry):
+            body(i)
+            return carry
+
+        lax.fori_loop(start, count, step, 0)
+
+    def wide(column):
+        return jnp.concatenate([column] * (pixels // column.shape[1]), axis=1)
+
+    def scatter(sems, src, dst):
+        def start(k):
+            d = lax.rem(rank + k, RANKS)
+            copy(src(d), dst, sems, k, (d, core)).start()
+
+        loop(RANKS, start, 1)
+
+    def arrived(sems, src, dst, then=None):
+        def wait(k):
+            s = lax.rem(rank + RANKS - k, RANKS)
+            copy(src(s), dst(s), sems, k, (s, core)).wait_recv()
+            if then is not None:
+                then(k, s)
+
+        loop(RANKS, wait, 1)
+
+    def scattered(sems, src, dst):
+        def wait(k):
+            d = lax.rem(rank + k, RANKS)
+            copy(src(d), dst, sems, k, (d, core)).wait_send()
+
+        loop(RANKS, wait, 1)
+
+    barrier = pltpu.get_barrier_semaphore()
+
+    def greet(k):
+        pl.semaphore_signal(
+            barrier, inc=1, device_id=(lax.rem(rank + k, RANKS), core), device_id_type=MESH
+        )
+
+    loop(RANKS, greet, 1)
+    pl.semaphore_signal(barrier, inc=1, device_id=twin, device_id_type=MESH)
+
+    def fetch_up(m):
+        cols = pl.ds(pl.multiple_of(m * part, part), part)
+        return pltpu.make_async_copy(v.w_up.at[:, cols], v.wu.at[m], v.fetch.at[0, m])
+
+    def fetch_down(m):
+        rows = pl.ds(pl.multiple_of(m * part, part), part)
+        return pltpu.make_async_copy(v.w_down.at[rows], v.wd.at[m], v.fetch.at[1, m])
+
+    def fetch(m):
+        fetch_up(m).start()
+        fetch_down(m).start()
+
+    loop(chunks, fetch)
+
+    for g in range(2):
+        v.tok[:, g * columns : (g + 1) * columns] = v.tokens[g, 0].astype(F32).T
+
+    def cut_tokens(d):
+        rows = v.tok[pl.ds(pl.multiple_of(d * own, 8), own), :]
+        both = jnp.concatenate([rows[:, :columns], rows[:, columns:]], axis=0)
+        v.tb[core, d] = both.astype(BF16)
+
+    loop(RANKS, cut_tokens)
+    lines = []
+    for vector in (v.b_up, v.skip_gain, v.ln_gain, v.ln_bias, v.layer_scale, v.b_down):
+        line = vector[...].reshape(1, vector.shape[0])
+        lines += [line[:, q * 128 : (q + 1) * 128] for q in range(vector.shape[0] // 128)]
+    lines.append(jnp.zeros((32 - len(lines), 128), F32))
+    v.vx[core] = jnp.concatenate(lines, axis=0)
+    pl.semaphore_wait(barrier, RANKS)
+    scatter(v.a1, lambda d: v.tb.at[core, d], v.rb1.at[rank])
+    v.rb1[rank] = v.tb[core, rank]
+    copy(v.tb.at[core], v.tb.at[core], v.tw, 0, twin).start()
+    copy(v.vx.at[core], v.vx.at[core], v.tw, 1, twin).start()
+
+    def spread(which, rows):
+        block = jnp.concatenate([rows, jnp.zeros((128 - rows.shape[0], 128), F32)], axis=0)
+        cols = block.T
+        for q in range(15):
+            v.vb[q // 3, which, q % 3 * 128 : (q % 3 + 1) * 128, :] = jnp.broadcast_to(
+                cols[:, 12 + q : 13 + q], (128, 128)
+            )
+        return cols
+
+    cols = spread(core, v.vx[core])
+    for m in range(chunks):
+        for q in range(2):
+            v.bias[m, q * 128 : (q + 1) * 128, :] = jnp.broadcast_to(
+                cols[:, 2 * m + q : 2 * m + q + 1], (128, 128)
+            )
+    for g in range(2):
+        v.cot[:, g * columns : (g + 1) * columns] = v.cotangent[g, 0].astype(F32).T
+    places_w = lax.broadcasted_iota(jnp.int32, (1, columns), 1)
+    inside = jnp.concatenate(
+        [(places_w < jnp.where(rank < heights[g], widths[g], 0)).astype(F32) for g in range(2)],
+        axis=1,
+    )
+    v.inside[...] = jnp.broadcast_to(inside, (8, pixels))
+
+    def mask_rows(q):
+        rows = pl.ds(pl.multiple_of(q * 128, 128), 128)
+        masked = v.cot[rows, :] * v.inside[0:1, :]
+        v.gb[core, rows, :] = (masked * wide(v.vb[3, core, rows, :])).astype(BF16)
+
+    loop(here // 128, mask_rows)
+    copy(v.gb.at[core], v.gb.at[core], v.tw, 2, twin).start()
+
+    lane = lax.broadcasted_iota(jnp.int32, (slab, lanes), 1) // per
+    row = lax.broadcasted_iota(jnp.int32, (slab, lanes), 0)
+    row = jnp.where(row >= own, row - own, row)
+    v.pick[...] = (lane == row).astype(F32)
+    chosen = lax.broadcasted_iota(jnp.int32, (here, lanes), 1) // per + rank * own
+    chosen = (lax.broadcasted_iota(jnp.int32, (here, lanes), 0) == chosen).astype(F32)
+    all_modes = jnp.concatenate(
+        [v.log_step[...], jnp.zeros((6, here), F32)]
+        + [v.log_decay[a] for a in range(2)]
+        + [v.frequency[a] for a in range(2)]
+        + [v.b_in[a, i] for i in range(2) for a in range(2)]
+        + [v.c_out[a, i] for i in range(2) for a in range(2)],
+        axis=0,
+    )
+    all_modes = jnp.dot(all_modes, chosen, precision=PRECISE, preferred_element_type=F32)
+    mode = lax.broadcasted_iota(jnp.int32, (per, lanes), 1) % per
+    mode = (mode == lax.broadcasted_iota(jnp.int32, (per, lanes), 0)).astype(F32)
+    v.of_mode[...] = mode
+    own_modes = jnp.sum(all_modes[8:].reshape(12, per, lanes) * mode[None], axis=1)
+    v.modes[...] = jnp.concatenate([all_modes[:2], own_modes, own_modes[:2]], axis=0)
+    mv = mode_values(v.modes[...])
+
+    def powers(axis, place):
+        angle = mv.step_im[axis : axis + 1] * place
+        fade = jnp.exp(mv.step_re[axis : axis + 1] * place)
+        return fade * jnp.cos(angle), fade * jnp.sin(angle)
+
+    high_place = lax.broadcasted_iota(jnp.int32, (RANKS, lanes), 0).astype(F32)
+    v.eh[0], v.eh[1] = powers(0, high_place)
+    low_place = lax.broadcasted_iota(jnp.int32, (8, lanes), 0).astype(F32)
+    base = powers(1, low_place)
+    many = columns // 8
+    v.ej[0], v.ej[1] = powers(
+        1, 8.0 * lax.broadcasted_iota(jnp.int32, (many, lanes), 0).astype(F32)
+    )
+    coef_w = tuple(2.0 * part_of[1:2] for part_of in mv.coef)
+
+    def fill(j):
+        at = pl.ds(pl.multiple_of(j * 8, 8), 8)
+        jump = (v.ej[0, pl.ds(j, 1), :], v.ej[1, pl.ds(j, 1), :])
+        e_re, e_im = times(base, jump)
+        v.ew[0, at, :] = e_re
+        v.ew[1, at, :] = e_im
+        v.kt[at, :] = coef_w[0] * e_re - coef_w[1] * e_im
+
+    loop(many, fill)
+    k_width = lax.dot_general(
+        v.pick[...], v.kt[...], NT, precision=PRECISE, preferred_element_type=F32
+    )
+    k_re = jnp.dot(k_width, v.to_re[...], precision=PRECISE, preferred_element_type=F32)
+    k_im = jnp.dot(k_width, v.to_im[...], precision=PRECISE, preferred_element_type=F32)
+    first_lane = lax.broadcasted_iota(jnp.int32, (slab, columns), 1) == 0
+    v.ks[0] = k_re
+    v.ks[1] = jnp.where(first_lane, 0.0, k_im)
+    v.ks[2] = jnp.where(first_lane, k_im, k_re)
+    coef_h = tuple(2.0 * part_of[0:1] for part_of in mv.coef)
+    v.kt[0:RANKS, :] = coef_h[0] * v.eh[0] - coef_h[1] * v.eh[1]
+
+    def k_height(l):
+        taps = jnp.sum(v.pick[...] * v.kt[pl.ds(l, 1), :], axis=1, keepdims=True)
+        v.kh[l] = jnp.broadcast_to(taps, (slab, 128))
+
+    loop(RANKS, k_height)
+
+    def turn(m):
+        fetch_up(m).wait()
+        fetch_down(m).wait()
+        v.wut[m] = v.wu[m].T
+        v.wdt[m] = v.wd[m].T
+
+    loop(chunks // 2, turn)
+
+    arrived(v.a1, lambda s: v.tb.at[core, s], lambda s: v.rb1.at[s])
+    step_rows = 4
+
+    def convolve(b):
+        at = pl.ds(b * step_rows, step_rows)
+        values = v.rb1[at].reshape(step_rows * slab, columns).astype(F32)
+        shape = (step_rows, slab, columns)
+        x_re = jnp.dot(values, v.to_re[...], precision=HIGH, preferred_element_type=F32)
+        x_im = jnp.dot(values, v.to_im[...], precision=HIGH, preferred_element_type=F32)
+        x_re, x_im = x_re.reshape(shape), x_im.reshape(shape)
+        v.xs[0, at] = x_re
+        v.xs[1, at] = x_im
+        k0, k1, k2 = v.ks[0], v.ks[1], v.ks[2]
+        y_re = (x_re * k0 - x_im * k1).reshape(step_rows * slab, columns)
+        y_im = (x_re * k1 + x_im * k2).reshape(step_rows * slab, columns)
+        along = jnp.dot(y_re, v.from_re[...], precision=HIGH, preferred_element_type=F32)
+        along += jnp.dot(y_im, v.from_im[...], precision=HIGH, preferred_element_type=F32)
+        v.along[at] = along.astype(BF16).astype(F32).reshape(shape)
+
+    loop(RANKS // step_rows, convolve)
+
+    def by_tiles(body):
+        def rows(r):
+            for half in range(columns // 128):
+                body(pl.ds(pl.multiple_of(r * 8, 8), 8), slice(half * 128, half * 128 + 128))
+
+        loop(slab // 8, rows)
+
+    def down_rows(at, cut):
+        taps = [v.kh[l, at, :] for l in range(RANKS)]
+        values = [v.along[i, at, cut] for i in range(RANKS)]
+        for i in range(RANKS):
+            total = taps[0] * values[i]
+            for l in range(1, i + 1):
+                total += taps[l] * values[i - l]
+            v.tall[i, at, cut] = total
+
+    by_tiles(down_rows)
+    v.sb2[...] = v.tall[...].astype(BF16)
+    scatter(v.a2, lambda d: v.sb2.at[d], v.rb2.at[core, rank])
+    v.rb2[core, rank] = v.sb2[rank]
+    copy(v.rb2.at[core, rank], v.rb2.at[core, rank], v.fw, 0, twin).start()
+
+    copy(v.vx.at[core], v.vx.at[1 - core], v.tw, 1, twin).wait_recv()
+    spread(1 - core, v.vx[1 - core])
+    loop(chunks, turn, chunks // 2)
+    v.branch[...] = jnp.zeros_like(v.branch)
+    v.gn[...] = jnp.zeros_like(v.gn)
+
+    def forward(k, s):
+        copy(v.rb2.at[core, s], v.rb2.at[core, s], v.fw, k, twin).start()
+
+    arrived(v.a2, lambda s: v.sb2.at[s], lambda s: v.rb2.at[core, s], forward)
+    copy(v.tb.at[core], v.tb.at[1 - core], v.tw, 0, twin).wait_recv()
+
+    def forwarded(k):
+        s = lax.rem(rank + RANKS - k, RANKS)
+        copy(v.rb2.at[core, s], v.rb2.at[1 - core, s], v.fw, k, twin).wait_recv()
+
+    loop(RANKS, forwarded)
+
+    eight = jnp.zeros((8, pixels), F32)
+
+    def folded(values):
+        return values.reshape(own // 8, 8, pixels).sum(axis=0)
+
+    def mix(i, total):
+        which, d = i // RANKS, lax.rem(i, RANKS)
+        spatial = v.rb2[which, d].astype(F32)
+        token = v.tb[which, d].astype(F32)
+        skip = wide(v.vb[0, which, pl.ds(pl.multiple_of(d * own, 8), own), :])
+        spatial = jnp.concatenate([spatial[:own], spatial[own:]], axis=1)
+        token = jnp.concatenate([token[:own], token[own:]], axis=1)
+        mixed = spatial + skip * token
+        v.xhat[i] = mixed
+        return total + folded(mixed)
+
+    channels = 2 * here
+    total = lax.fori_loop(0, 2 * RANKS, mix, eight)
+    centre = jnp.sum(total, axis=0, keepdims=True) * (1.0 / channels)
+
+    def squares(i, total):
+        off = v.xhat[i] - centre
+        return total + folded(off * off)
+
+    total = lax.fori_loop(0, 2 * RANKS, squares, eight)
+    spread_of = jnp.sum(total, axis=0, keepdims=True) * (1.0 / channels)
+    inv_std = lax.rsqrt(spread_of + EPSILON)
+    v.inv[...] = jnp.broadcast_to(inv_std, (8, pixels))
+
+    def normalize(q):
+        rows = []
+        for k in range(2):
+            i = 2 * q + k
+            which, d = i // RANKS, lax.rem(i, RANKS)
+            at = pl.ds(pl.multiple_of(d * own, 8), own)
+            x_hat = (v.xhat[i] - centre) * inv_std
+            v.xhat[i] = x_hat
+            rows.append(x_hat * wide(v.vb[1, which, at, :]) + wide(v.vb[2, which, at, :]))
+        at = pl.ds(pl.multiple_of(q * 2 * own, 16), 2 * own)
+        v.normed[at, :] = jnp.concatenate(rows, axis=0).astype(BF16)
+
+    loop(RANKS, normalize)
+    copy(v.gb.at[core], v.gb.at[1 - core], v.tw, 2, twin).wait_recv()
+
+    def feed(t):
+        normed = v.normed[...]
+        g_branch = v.gb[...].reshape(channels, pixels)
+        hidden = jnp.dot(v.wut[t], normed, preferred_element_type=F32) + wide(v.bias[t])
+        phi = 0.5 + 0.5 * lax.erf(hidden * (0.5**0.5))
+        density = jnp.exp(-0.5 * hidden * hidden) * ((2.0 * jnp.pi) ** -0.5)
+        active = (hidden * phi).astype(BF16)
+        slope = phi + hidden * density
+        g_active = jnp.dot(v.wd[t], g_branch, preferred_element_type=F32)
+        g_hidden = (g_active * slope).astype(BF16)
+        down = lax.dot_general(active, g_branch, NT, preferred_element_type=F32)
+        v.pd[t] = down.astype(BF16).reshape(2, 2, part // 4, channels)
+        up = lax.dot_general(normed, g_hidden, NT, preferred_element_type=F32)
+        v.pu[t] = up.astype(BF16).reshape(2, 2, channels // 4, part)
+        v.gn[...] += jnp.dot(v.wu[t], g_hidden, preferred_element_type=F32)
+        v.branch[...] += jnp.dot(v.wdt[t], active, preferred_element_type=F32)
+        ones = jnp.ones((8, pixels), BF16)
+        v.dbu[t] = lax.dot_general(ones, g_hidden, NT, preferred_element_type=F32)
+
+    def share():
+        v.gn_out[...] = v.gn[...].astype(BF16)
+        copy(v.gn_out, v.gn_in, v.tw, 3, twin).start()
+        theirs = pl.ds(pl.multiple_of((1 - core) * here, here), here)
+        v.br_out[...] = v.branch[theirs, :].astype(BF16)
+        copy(v.br_out, v.br_in, v.tw, 4, twin).start()
+
+    def lane_sum(values):
+        return sum(values[:, q * 128 : (q + 1) * 128] for q in range(pixels // 128))
+
+    def norm_back():
+        copy(v.gn_out, v.gn_in, v.tw, 3, twin).wait_recv()
+
+        def whole(q, totals):
+            at = pl.ds(pl.multiple_of(q * 2 * own, 16), 2 * own)
+            g_normed = v.gn[at, :] + v.gn_in[at, :].astype(F32)
+            v.gn[at, :] = g_normed
+            one, two = totals
+            for k in range(2):
+                i = 2 * q + k
+                which, d = i // RANKS, lax.rem(i, RANKS)
+                gain = wide(v.vb[1, which, pl.ds(pl.multiple_of(d * own, 8), own), :])
+                g_hat = g_normed[k * own : (k + 1) * own] * gain
+                one = one + folded(g_hat)
+                two = two + folded(g_hat * v.xhat[i])
+            return one, two
+
+        one, two = lax.fori_loop(0, RANKS, whole, (eight, eight))
+        one = jnp.sum(one, axis=0, keepdims=True) * (1.0 / channels)
+        two = jnp.sum(two, axis=0, keepdims=True) * (1.0 / channels)
+        scale = v.inv[0:1, :]
+
+        def each(d):
+            at = pl.ds(pl.multiple_of(d * own, 8), own)
+            x_hat = v.xhat[core * RANKS + d]
+            g_normed = v.gn[pl.ds(pl.multiple_of(core * here + d * own, 8), own), :]
+            g_mixed = scale * (g_normed * wide(v.vb[1, core, at, :]) - one - x_hat * two)
+            v.gmix[at, :] = g_mixed
+            v.sums[0, at, :] = lane_sum(g_mixed * v.tok[at, :])
+            v.sums[1, at, :] = lane_sum(g_normed * x_hat)
+            v.sums[2, at, :] = lane_sum(g_normed)
+            both = jnp.concatenate([g_mixed[:, :columns], g_mixed[:, columns:]], axis=0)
+            v.sb3[d] = both.astype(BF16)
+
+        loop(RANKS, each)
+        scatter(v.a3, lambda d: v.sb3.at[d], v.rb3.at[rank])
+        v.rb3[rank] = v.sb3[rank]
+
+    def outputs():
+        copy(v.br_out, v.br_in, v.tw, 4, twin).wait_recv()
+        mask = v.inside[0:1, :]
+
+        def rows(q):
+            at = pl.ds(pl.multiple_of(q * 128, 128), 128)
+            branch = v.branch[pl.ds(pl.multiple_of(core * here + q * 128, 128), 128), :]
+            branch = branch + v.br_in[at, :].astype(F32) + wide(v.vb[4, core, at, :])
+            masked = branch * mask
+            v.sums[3, at, :] = lane_sum(v.gb[core, at, :].astype(F32))
+            v.sums[4, at, :] = lane_sum(masked * v.cot[at, :])
+            v.res[at, :] = v.tok[at, :] + masked * wide(v.vb[3, core, at, :])
+
+        loop(here // 128, rows)
+        for g in range(2):
+            v.output[g, 0] = v.res[:, g * columns : (g + 1) * columns].T.astype(BF16)
+
+    def convolve_back():
+        arrived(v.a3, lambda s: v.sb3.at[s], lambda s: v.rb3.at[s])
+        v.tall[...] = v.rb3[...].astype(F32)
+
+        def up_rows(at, cut):
+            taps = [v.kh[l, at, :] for l in range(RANKS)]
+            values = [v.tall[i, at, cut] for i in range(RANKS)]
+            for i in range(RANKS):
+                total = taps[0] * values[i]
+                for l in range(1, RANKS - i):
+                    total += taps[l] * values[i + l]
+                v.galong[i, at, cut] = total.astype(BF16).astype(F32)
+
+        by_tiles(up_rows)
+
+        def lag_rows(at, cut):
+            grads = [v.tall[i, at, cut] for i in range(RANKS)]
+            values = [v.along[i, at, cut] for i in range(RANKS)]
+            for l in range(RANKS):
+                total = grads[l] * values[0]
+                for i in range(l + 1, RANKS):
+                    total += grads[i] * values[i - l]
+                v.lags[l, at, cut] = total
+
+        by_tiles(lag_rows)
+        none = jnp.zeros((slab, columns), F32)
+
+        def one_step(b, totals):
+            at = pl.ds(b * step_rows, step_rows)
+            shape = (step_rows, slab, columns)
+            values = v.galong[at].reshape(step_rows * slab, columns)
+            g_re = jnp.dot(values, v.to_re[...], precision=HIGH, preferred_element_type=F32)
+            g_im = jnp.dot(values, v.to_im[...], precision=HIGH, preferred_element_type=F32)
+            g_re, g_im = g_re.reshape(shape), g_im.reshape(shape)
+            x_re, x_im = v.xs[0, at], v.xs[1, at]
+            k0, k1, k2 = v.ks[0], v.ks[1], v.ks[2]
+            y_re = (g_re * k0 + g_im * k1).reshape(step_rows * slab, columns)
+            y_im = (g_im * k2 - g_re * k1).reshape(step_rows * slab, columns)
+            conv = jnp.dot(y_re, v.from_re[...], precision=HIGH, preferred_element_type=F32)
+            conv += jnp.dot(y_im, v.from_im[...], precision=HIGH, preferred_element_type=F32)
+            v.sb4[at] = conv.reshape(shape).astype(BF16)
+            return (
+                totals[0] + (x_re * g_re).sum(axis=0),
+                totals[1] + (x_im * g_im).sum(axis=0),
+                totals[2] + (x_re * g_im - x_im * g_re).sum(axis=0),
+            )
+
+        cross = lax.fori_loop(0, RANKS // step_rows, one_step, (none, none, none))
+        scatter(v.a4, lambda d: v.sb4.at[d], v.rb4.at[rank])
+        v.rb4[rank] = v.sb4[rank]
+        zero_lane = lax.broadcasted_iota(jnp.int32, (slab, columns), 1) == 0
+        c_re = cross[0] + jnp.where(zero_lane, 0.0, cross[1])
+        c_im = jnp.where(zero_lane, cross[1], cross[2])
+        dk_width = jnp.dot(c_re, v.from_re[...], precision=PRECISE, preferred_element_type=F32)
+        dk_width += jnp.dot(c_im, v.from_im[...], precision=PRECISE, preferred_element_type=F32)
+        v.kt[...] = lax.dot_general(
+            dk_width, v.pick[...], TN, precision=PRECISE, preferred_element_type=F32
+        )
+
+        def lag_height(l):
+            at = pl.ds(l, 1)
+            lag = jnp.sum(v.lags[l], axis=1, keepdims=True)
+            v.kth[at, :] = jnp.sum(lag * v.pick[...], axis=0, keepdims=True)
+
+        loop(RANKS, lag_height)
+        parameters()
+
+    def parameters():
+        def moments(dk, e_re, e_im):
+            place = lax.broadcasted_iota(jnp.int32, dk.shape, 0).astype(F32)
+            terms = (dk * e_re, dk * e_im)
+            plain = [jnp.sum(term, axis=0, keepdims=True) for term in terms]
+            timed = [jnp.sum(term * place, axis=0, keepdims=True) for term in terms]
+            return plain + timed
+
+        rows_h = moments(v.kth[...], v.eh[0], v.eh[1])
+        rows_w = moments(v.kt[...], v.ew[0], v.ew[1])
+        p_re, p_im, t_re, t_im = (
+            2.0 * jnp.concatenate([h, w], axis=0) for h, w in zip(rows_h, rows_w)
+        )
+        plain, timed = (p_re, p_im), (t_re, t_im)
+        mv = mode_values(v.modes[...])
+        step, rate = mv.step, mv.rate
+        zoh_plain = times(mv.zoh, plain)
+        g_b = times(mv.c, zoh_plain)
+        g_c = times(mv.b, zoh_plain)
+        coef_timed = times(mv.coef, timed)
+        prod_plain = times(mv.prod, plain)
+        slope = times(
+            (step * mv.once[0] - mv.zoh[0], step * mv.once[1] - mv.zoh[1]), mv.over
+        )
+        g_rate = times(prod_plain, slope)
+        g_rate = (g_rate[0] + step * coef_timed[0], g_rate[1] + step * coef_timed[1])
+        g_step = times(prod_plain, mv.once)[0] + times(coef_timed, rate)[0]
+        rows = [
+            step * g_step,
+            g_rate[0] * rate[0],
+            -g_rate[1],
+            g_b[0],
+            -g_b[1],
+            g_c[0],
+            -g_c[1],
+            jnp.zeros_like(step),
+        ]
+        table = jnp.concatenate(rows, axis=0)
+        z, y, x = rank // 4, (rank // 2) % 2, rank % 2
+        for five in range(3):
+            block = jnp.zeros((per, 128), F32)
+            for k in range(5 if five < 2 else 4):
+                r = 5 * five + k
+                at = lax.broadcasted_iota(jnp.int32, (128, lanes), 0) - k * own
+                at = (at == lax.broadcasted_iota(jnp.int32, (128, lanes), 1) // per).astype(BF16)
+                values = (v.of_mode[...] * table[r : r + 1]).astype(BF16)
+                block += lax.dot_general(values, at, NT, preferred_element_type=F32)
+            v.pack[five * per : (five + 1) * per, :] = block.astype(BF16)
+        ones = jnp.ones((8, 128), F32)
+        vectors = [
+            v.dbu[m, 0:1, q * 128 : (q + 1) * 128] for m in range(chunks) for q in range(part // 128)
+        ]
+        for k in range(5):
+            line = lax.dot_general(
+                ones, v.sums[k], NT, precision=PRECISE, preferred_element_type=F32
+            )
+            vectors += [line[0:1, q * 128 : (q + 1) * 128] for q in range(here // 128)]
+        vectors.append(jnp.zeros((32 - len(vectors), 128), F32))
+        v.pack[3 * per :, :] = jnp.concatenate(vectors, axis=0).astype(BF16)
+        v.gathered[z, y, x] = v.pack[...]
+
+        def to(k):
+            target = (lax.rem(z + k, 4) * 4 + y * 2 + x, core)
+            copy(v.pack, v.gathered.at[z, y, x], v.ga, k, target).start()
+
+        loop(4, to, 1)
+
+    def gather_across():
+        def wait(k):
+            s = lax.rem(z + 4 - k, 4)
+            copy(v.pack, v.gathered.at[s, y, x], v.ga, k, (s * 4 + y * 2 + x, core)).wait_recv()
+
+        loop(4, wait, 1)
+        mine = v.gathered.at[:, y, x]
+        copy(mine, mine, v.ga, 4, across).start()
+
+    def gather_beside():
+        theirs = v.gathered.at[:, 1 - y, x]
+        copy(theirs, theirs, v.ga, 4, across).wait_recv()
+        mine = v.gathered.at[:, :, x]
+        copy(mine, mine, v.ga, 5, beside).start()
+
+    def token_grads():
+        arrived(v.a4, lambda s: v.sb4.at[s], lambda s: v.rb4.at[s])
+
+        def rows(d):
+            at = pl.ds(pl.multiple_of(d * own, 8), own)
+            conv = v.rb4[d].astype(F32)
+            conv = jnp.concatenate([conv[:own], conv[own:]], axis=1)
+            skip = wide(v.vb[0, core, at, :])
+            v.res[at, :] = v.cot[at, :] + skip * v.gmix[at, :] + conv
+
+        loop(RANKS, rows)
+        for g in range(2):
+            v.d_tokens[g, 0] = v.res[:, g * columns : (g + 1) * columns].T.astype(BF16)
+
+    down = (v.pd, v.d1, v.d2, v.d3, v.d4, v.fd, v.d_sems.at[0], v.d_sems.at[1])
+    up = (v.pu, v.u1, v.u2, v.u3, v.u4, v.fu, v.u_sems.at[0], v.u_sems.at[1])
+
+    def leave(c):
+        return (
+            pltpu.make_async_copy(v.fd.at[c], v.down.at[c], v.leave.at[0, c]),
+            pltpu.make_async_copy(v.fu.at[c], v.up.at[c], v.leave.at[1, c]),
+        )
+
+    events = {
+        chunks: norm_back,
+        chunks + 1: outputs,
+        chunks + 3: convolve_back,
+        chunks + 4: gather_across,
+        chunks + 5: gather_beside,
+        chunks + 6: token_grads,
+    }
 
     def tick(t, carry):
-        for stage in range(STAGES):
+        @pl.when(t < chunks)
+        def _():
+            feed(t)
+
+        pl.when(t == chunks - 1)(share)
+        for when, event in events.items():
+            pl.when(t == when)(event)
+        for stage in range(STAGES - 1, -1, -1):
             c = t - stage
-
-            live = (c * (count - 1 - c) >= 0).astype(jnp.int32)
+            live = (c * (chunks - 1 - c) >= 0).astype(jnp.int32)
             role = live * (1 + middle)
             reduce_stage(stage, c, role, places, x, beside, across, down)
             reduce_stage(stage, c, role, places, y, across, beside, up)
+            if stage == STAGES - 1:
+
+                @pl.when(live > 0)
+                def _():
+                    for one in leave(c):
+                        one.start()
 
         return carry
 
-    lax.fori_loop(0, count + STAGES - 1, tick, 0)
-
-
-def reduce_scratch(shape):
-    count, _, _, rows, columns = shape
-    return [
-        pltpu.VMEM((count, 2, rows, columns), jnp.bfloat16),
-        pltpu.VMEM((count, 2, rows, columns), jnp.bfloat16),
-        pltpu.VMEM((count, rows, columns), jnp.bfloat16),
-        pltpu.VMEM((count, rows, columns), jnp.bfloat16),
-        pltpu.SemaphoreType.DMA((9, count)),
-        pltpu.SemaphoreType.DMA((9, count)),
-    ]
-
-
-def sum_weights(d_w_down, d_w_up, part):
-    hidden, channels = d_w_down.shape
-    count = hidden // part
-    down = d_w_down.astype(jnp.bfloat16).reshape(count, 2, 2, part // 4, channels)
-    up = d_w_up.astype(jnp.bfloat16).reshape(channels, count, part)
-    up = up.transpose(1, 0, 2).reshape(count, 2, 2, channels // 4, part)
+    lax.fori_loop(0, chunks + STAGES - 1, tick, 0)
+
+    theirs = v.gathered.at[:, :, 1 - x]
+    copy(theirs, theirs, v.ga, 5, beside).wait_recv()
+
+    def left(c):
+        for one in leave(c):
+            one.wait()
+
+    loop(chunks, left)
+    scattered(v.a1, lambda d: v.tb.at[core, d], v.rb1.at[rank])
+    scattered(v.a2, lambda d: v.sb2.at[d], v.rb2.at[core, rank])
+    scattered(v.a3, lambda d: v.sb3.at[d], v.rb3.at[rank])
+    scattered(v.a4, lambda d: v.sb4.at[d], v.rb4.at[rank])
+    copy(v.tb.at[core], v.tb.at[core], v.tw, 0, twin).wait_send()
+    copy(v.vx.at[core], v.vx.at[core], v.tw, 1, twin).wait_send()
+    copy(v.gb.at[core], v.gb.at[core], v.tw, 2, twin).wait_send()
+    copy(v.gn_out, v.gn_in, v.tw, 3, twin).wait_send()
+    copy(v.br_out, v.br_in, v.tw, 4, twin).wait_send()
+
+    def forward_sent(k):
+        s = lax.rem(rank + RANKS - k, RANKS)
+        copy(v.rb2.at[core, s], v.rb2.at[core, s], v.fw, k, twin).wait_send()
+
+    loop(RANKS, forward_sent)
+
+    def gather_sent(k):
+        target = (lax.rem(z + k, 4) * 4 + y * 2 + x, core)
+        copy(v.pack, v.gathered.at[z, y, x], v.ga, k, target).wait_send()
+
+    loop(4, gather_sent, 1)
+    mine = v.gathered.at[:, y, x]
+    copy(mine, mine, v.ga, 4, across).wait_send()
+    mine = v.gathered.at[:, :, x]
+    copy(mine, mine, v.ga, 5, beside).wait_send()
+
+
+def finish_kernel(own, down, up, gathered, output, d_tokens, *outs):
+    d_w_down, d_w_up, output_out, d_tokens_out = outs[:4]
+    d_log_step, d_log_decay, d_frequency, d_b_in, d_c_out = outs[4:9]
+    d_w_down[...] = down[...].reshape(d_w_down.shape).astype(F32)
+    d_w_up[...] = up[...].reshape(d_w_up.shape).astype(F32)
+    per, here = d_log_decay.shape[1:]
+
+    @pl.when(pl.program_id(0) == 0)
+    def _():
+        output_out[...] = output[...]
+        d_tokens_out[...] = d_tokens[...]
+        lane = lax.broadcasted_iota(jnp.int32, (per, 128), 1)
+        whole = []
+        for r in range(14):
+            five, k = divmod(r, 5)
+            windows = [jnp.zeros((per, 128), F32) for _ in range(here // 128)]
+            for s in range(RANKS):
+                block = gathered[s // 4, s // 2 % 2, s % 2, five * per : (five + 1) * per, :]
+                turned = pltpu.roll(block.astype(F32), (own * (s - k)) % 128, 1)
+                window, low = divmod(own * s, 128)
+                inside = (lane >= low) & (lane < low + own)
+                windows[window] = jnp.where(inside, turned, windows[window])
+                if low + own > 128:
+                    inside = lane < low + own - 128
+                    windows[window + 1] = jnp.where(inside, turned, windows[window + 1])
+            whole.append(jnp.concatenate(windows, axis=1))
+        for a in range(2):
+            d_log_step[a : a + 1, :] = jnp.sum(whole[a], axis=0, keepdims=True)
+            d_log_decay[a] = whole[2 + a]
+            d_frequency[a] = whole[4 + a]
+            for i in range(2):
+                d_b_in[a, i] = whole[6 + 2 * i + a]
+                d_c_out[a, i] = whole[10 + 2 * i + a]
+        sums = jnp.zeros((32, 128), F32)
+        for s in range(RANKS):
+            sums += gathered[s // 4, s // 2 % 2, s % 2, 3 * per :, :].astype(F32)
+        row = 0
+        for vector in outs[9:]:
+            for q in range(vector.shape[0] // 128):
+                vector[pl.ds(q * 128, 128)] = sums[row]
+                row += 1
+
+
+def block_shards(
+    tokens,
+    heights,
+    widths,
+    log_step,
+    log_decay,
+    frequency,
+    b_in,
+    c_out,
+    skip_gain,
+    ln_gain,
+    ln_bias,
+    w_up,
+    b_up,
+    w_down,
+    b_down,
+    layer_scale,
+    cotangent,
+):
+    columns, here = tokens.shape[2:]
+    modes_each = log_decay.shape[2]
+    hidden = w_up.shape[1]
+    own = here // RANKS
+    chunks = hidden // 256
+    part = hidden // chunks
+    channels = 2 * here
+    pixels = 2 * columns
+    lanes = own * modes_each
+    tables = spectral_tables(columns)
+    slabs = (RANKS, 2 * own, columns)
+    tall = pltpu.VMEM(slabs, F32)
     in_vmem = pl.BlockSpec(memory_space=pltpu.VMEM)
-    down, up = pl.pallas_call(
-        reduce_kernel,
-        out_shape=(
-            jax.ShapeDtypeStruct(down.shape, down.dtype),
-            jax.ShapeDtypeStruct(up.shape, up.dtype),
+    in_smem = pl.BlockSpec(memory_space=pltpu.SMEM)
+    anywhere = pl.BlockSpec(memory_space=pl.ANY)
+    inputs = dict(
+        tokens=(tokens, in_vmem),
+        cotangent=(cotangent, in_vmem),
+        heights=(heights, in_smem),
+        widths=(widths, in_smem),
+        log_step=(log_step, in_vmem),
+        log_decay=(log_decay.swapaxes(-1, -2), in_vmem),
+        frequency=(frequency.swapaxes(-1, -2), in_vmem),
+        b_in=(b_in.swapaxes(-1, -2), in_vmem),
+        c_out=(c_out.swapaxes(-1, -2), in_vmem),
+        b_up=(b_up, in_vmem),
+        skip_gain=(skip_gain, in_vmem),
+        ln_gain=(ln_gain, in_vmem),
+        ln_bias=(ln_bias, in_vmem),
+        layer_scale=(layer_scale, in_vmem),
+        b_down=(b_down, in_vmem),
+        w_up=(w_up, anywhere),
+        w_down=(w_down, anywhere),
+        to_re=(tables[0], in_vmem),
+        to_im=(tables[1], in_vmem),
+        from_re=(tables[2], in_vmem),
+        from_im=(tables[3], in_vmem),
+    )
+    down_shape = (chunks, 2, 2, part // 4, channels)
+    up_shape = (chunks, 2, 2, channels // 4, part)
+    outs = dict(
+        output=(jax.ShapeDtypeStruct(tokens.shape, BF16), in_vmem),
+        d_tokens=(jax.ShapeDtypeStruct(tokens.shape, BF16), in_vmem),
+        down=(jax.ShapeDtypeStruct(down_shape, BF16), anywhere),
+        up=(jax.ShapeDtypeStruct(up_shape, BF16), anywhere),
+        gathered=(jax.ShapeDtypeStruct((4, 2, 2, 3 * modes_each + 32, 128), BF16), in_vmem),
+    )
+    low_slabs = pltpu.VMEM(slabs, BF16)
+    both_slabs = pltpu.VMEM((2,) + slabs, BF16)
+    scratch = dict(
+        wu=pltpu.VMEM((chunks, channels, part), BF16),
+        wd=pltpu.VMEM((chunks, part, channels), BF16),
+        wut=pltpu.VMEM((chunks, part, channels), BF16),
+        wdt=pltpu.VMEM((chunks, channels, part), BF16),
+        tok=pltpu.VMEM((here, pixels), F32),
+        cot=pltpu.VMEM((here, pixels), F32),
+        gmix=pltpu.VMEM((here, pixels), F32),
+        res=pltpu.VMEM((here, pixels), F32),
+        tb=both_slabs,
+        rb1=low_slabs,
+        sb2=low_slabs,
+        rb2=both_slabs,
+        sb3=low_slabs,
+        rb3=low_slabs,
+        sb4=low_slabs,
+        rb4=low_slabs,
+        vx=pltpu.VMEM((2, 32, 128), F32),
+        vb=pltpu.VMEM((5, 2, here, 128), F32),
+        bias=pltpu.VMEM((chunks, part, 128), F32),
+        inside=pltpu.VMEM((8, pixels), F32),
+        inv=pltpu.VMEM((8, pixels), F32),
+        gb=pltpu.VMEM((2, here, pixels), BF16),
+        modes=pltpu.VMEM((16, lanes), F32),
+        of_mode=pltpu.VMEM((modes_each, lanes), F32),
+        pick=pltpu.VMEM((2 * own, lanes), F32),
+        eh=pltpu.VMEM((2, RANKS, lanes), F32),
+        ej=pltpu.VMEM((2, columns // 8, lanes), F32),
+        ew=pltpu.VMEM((2, columns, lanes), F32),
+        kt=pltpu.VMEM((columns, lanes), F32),
+        kth=pltpu.VMEM((RANKS, lanes), F32),
+        ks=pltpu.VMEM((3, 2 * own, columns), F32),
+        kh=pltpu.VMEM((RANKS, 2 * own, 128), F32),
+        xs=pltpu.VMEM((2,) + slabs, F32),
+        along=tall,
+        tall=tall,
+        galong=tall,
+        lags=tall,
+        xhat=pltpu.VMEM((2 * RANKS, own, pixels), F32),
+        normed=pltpu.VMEM((channels, pixels), BF16),
+        branch=pltpu.VMEM((channels, pixels), F32),
+        gn=pltpu.VMEM((channels, pixels), F32),
+        gn_out=pltpu.VMEM((channels, pixels), BF16),
+        gn_in=pltpu.VMEM((channels, pixels), BF16),
+        br_out=pltpu.VMEM((here, pixels), BF16),
+        br_in=pltpu.VMEM((here, pixels), BF16),
+        dbu=pltpu.VMEM((chunks, 8, part), F32),
+        sums=pltpu.VMEM((5, here, 128), F32),
+        pack=pltpu.VMEM((3 * modes_each + 32, 128), BF16),
+        fetch=pltpu.SemaphoreType.DMA((2, chunks)),
+        leave=pltpu.SemaphoreType.DMA((2, chunks)),
+    )
+
+    def reduction(shape):
+        count, halves, pieces, rows, width = shape
+        whole = pltpu.VMEM(shape, BF16)
+        half = pltpu.VMEM((count, pieces, rows, width), BF16)
+        piece = pltpu.VMEM((count, rows, width), BF16)
+        return whole, half, half, piece, piece, whole, pltpu.SemaphoreType.DMA((2, 9, count))
+
+    down_scratch, up_scratch = reduction(down_shape), reduction(up_shape)
+    scratch.update(
+        zip(("pd", "d1", "d2", "d3", "d4", "fd", "d_sems"), down_scratch),
+    )
+    scratch.update(
+        zip(("pu", "u1", "u2", "u3", "u4", "fu", "u_sems"), up_scratch),
+    )
+    several = pltpu.SemaphoreType.DMA((2, RANKS))
+    scratch.update(a1=several, a2=several, a3=several, a4=several, fw=several)
+    scratch.update(tw=pltpu.SemaphoreType.DMA((2, 5)), ga=pltpu.SemaphoreType.DMA((2, 6)))
+    names = tuple(inputs) + tuple(outs) + tuple(scratch)
+    output, d_tokens, down, up, gathered = pl.pallas_call(
+        functools.partial(block_kernel, names),
+        out_shape=tuple(shape for shape, _ in outs.values()),
+        in_specs=[spec for _, spec in inputs.values()],
+        out_specs=tuple(spec for _, spec in outs.values()),
+        scratch_shapes=list(scratch.values()),
+        compiler_params=pltpu.CompilerParams(
+            collective_id=0, has_side_effects=True, vmem_limit_bytes=62 << 20
         ),
-        in_specs=[in_vmem] * 2,
-        out_specs=(in_vmem, in_vmem),
-        scratch_shapes=reduce_scratch(down.shape) + reduce_scratch(up.shape),
-        compiler_params=pltpu.CompilerParams(
-            collective_id=0, has_side_effects=True, vmem_limit_bytes=48 << 20
-        ),
-    )(down, up)
-    up = up.reshape(count, channels, part).transpose(1, 0, 2).reshape(channels, hidden)
-    return down.reshape(hidden, channels).astype(jnp.float32), up.astype(jnp.float32)
+    )(*(value for value, _ in inputs.values()))
+    def fixed(shape):
+        return pl.BlockSpec(shape, lambda m, rank=len(shape): (0,) * rank)
+
+    result = (
+        jax.ShapeDtypeStruct((hidden, channels), F32),
+        jax.ShapeDtypeStruct((channels, hidden), F32),
+        output,
+        d_tokens,
+        log_step,
+        jax.ShapeDtypeStruct((2, modes_each, here), F32),
+        jax.ShapeDtypeStruct((2, modes_each, here), F32),
+        jax.ShapeDtypeStruct((2, 2, modes_each, here), F32),
+        jax.ShapeDtypeStruct((2, 2, modes_each, here), F32),
+        b_up,
+        skip_gain,
+        ln_gain,
+        ln_bias,
+        b_down,
+        layer_scale,
+    )
+    result = tuple(jax.ShapeDtypeStruct(one.shape, one.dtype) for one in result)
+    (
+        d_w_down,
+        d_w_up,
+        output,
+        d_tokens,
+        d_log_step,
+        d_log_decay,
+        d_frequency,
+        d_b_in,
+        d_c_out,
+        d_b_up,
+        d_skip_gain,
+        d_ln_gain,
+        d_ln_bias,
+        d_b_down,
+        d_layer_scale,
+    ) = pl.pallas_call(
+        functools.partial(finish_kernel, own),
+        grid=(chunks,),
+        out_shape=result,
+        in_specs=[
+            pl.BlockSpec((1,) + down_shape[1:], lambda m: (m, 0, 0, 0, 0)),
+            pl.BlockSpec((1,) + up_shape[1:], lambda m: (m, 0, 0, 0, 0)),
+            fixed(gathered.shape),
+            fixed(tokens.shape),
+            fixed(tokens.shape),
+        ],
+        out_specs=(
+            pl.BlockSpec((part, channels), lambda m: (m, 0)),
+            pl.BlockSpec((channels, part), lambda m: (0, m)),
+        )
+        + tuple(fixed(one.shape) for one in result[2:]),
+        compiler_params=pltpu.CompilerParams(vmem_limit_bytes=62 << 20),
+    )(down, up, gathered, output, d_tokens)
+    return (
+        output,
+        d_tokens,
+        d_log_step,
+        d_log_decay.swapaxes(-1, -2),
+        d_frequency.swapaxes(-1, -2),
+        d_b_in.swapaxes(-1, -2),
+        d_c_out.swapaxes(-1, -2),
+        d_skip_gain,
+        d_ln_gain,
+        d_ln_bias,
+        d_w_up,
+        d_b_up,
+        d_w_down,
+        d_b_down,
+        d_layer_scale,
+    )
 
 
 def shards(
@@ -439,12 +1321,9 @@
         gathered(pair, dim_num)
         for pair, dim_num in zip(zip(height_grads, width_grads), (1, 1, 1, 2, 2))
     )
-    if row_count == 16:
-        d_w_down, d_w_up = sum_weights(d_w_down, d_w_up, w_up.shape[1] // 12)
-    else:
-        d_w_down, d_w_up = lax.psum((d_w_down, d_w_up), "rows")
-    d_skip_gain, d_ln_gain, d_ln_bias, d_b_up, d_b_down, d_layer_scale = lax.psum(
-        (d_skip_gain, d_ln_gain, d_ln_bias, d_b_up, d_b_down, d_layer_scale), "rows"
+    d_w_down, d_w_up, d_skip_gain, d_ln_gain, d_ln_bias, d_b_up, d_b_down, d_layer_scale = lax.psum(
+        (d_w_down, d_w_up, d_skip_gain, d_ln_gain, d_ln_bias, d_b_up, d_b_down, d_layer_scale),
+        "rows",
     )
     return (output, d_tokens) + param_grads + (
         d_skip_gain,
@@ -459,8 +1338,9 @@
 
 
 def solution(mesh):
+    one_row_each = mesh.shape["rows"] == RANKS and mesh.shape["ch"] == 2
     return jax.shard_map(
-        shards,
+        block_shards if one_row_each else shards,
         mesh=mesh,
         in_specs=(
             P(None, "rows", None, "ch"),

time: 575 us -> 156 us (0.27)
  blocking collectives: 289 us -> 0 us
  Pallas kernels: 86.4 us -> 155 us
  matrix products: 60.7 us -> 0 us
  local copies, waits for them, and re-layouts: 51.8 us -> 0 us
  other arithmetic: 39.5 us -> 0 us
  starting transfers between devices: 23 us -> 0 us
  between operations: 16 us -> 0.82 us
    all_gather x7 -> x0, blocking collectives: 206 us -> none  [the longest x5 201 us: gathered(): return lax.all_gather(jnp.stack(pieces), 'rows', axis=dim_num, tiled=True)]
    psum x3 -> x0, blocking collectives: 83.5 us -> none  [the longest x1 77.2 us: shards(): lax.psum((d_skip_gain, d_ln_gain, d_ln_bias, d_b_up, d_b_down, d_layer_sc...]
    pallas_call x1 -> x2, Pallas kernels: 86.4 us -> 155 us  [the longest x1 146 us: block_shards(): pl.pallas_call(functools.partial(block_kernel, names), out_shape=tuple((s...]
    dot_general x30 -> x0, matrix products: 60.7 us -> none  [the longest x1 10 us: shards(): lax.dot_general(g_branch_all, w_down, over_cols, preferred_element_type=j...]
    unnamed x239 -> x0, local copies, waits for them, and re-layouts: 27.2 us -> none
    all_to_all x4 -> x0, starting transfers between devices: 22.9 us -> none  [the longest x1 8.31 us: shards(): lax.all_to_all(tokens, 'rows', split_axis=3, concat_axis=1, tiled=True)]
    reduce_sum x10 -> x0, other arithmetic: 19.9 us -> none  [the longest x2 5.6 us: make_kernel(): fading = jnp.exp(step_re[None] * places)]
    convert_element_type x11 -> x0, other arithmetic: 13.4 us -> none  [the longest x1 4.28 us: sum_weights(): up.astype(jnp.float32)]
  transfers between devices with their start and end apart: 6 -> 0, of which waited for: 1 -> 0; matrix products, arithmetic and copies ran while one was open for 12% -> 0% of each run, Pallas kernels for 15% -> 0%
where the time goes in v2:
time: 156 us; the launch traced here: 155 us
  Pallas kernels  155 us (99%)
    pallas_call x1, Pallas kernels, block_shards(): pl.pallas_call(functools.partial(block_kernel, names), out_shape=tuple((s...  146 us
    pallas_call x1, Pallas kernels, block_shards(): pl.pallas_call(functools.partial(finish_kernel, own), grid=(chunks,), out...  8.22 us

profile of v2, /device:TPU:0, one launch (start us, length us, event | category | flops | bytes accessed | tf_op | source)
XLA Modules:
  0.0 155.5 jit_solution(2564386685478026320)
XLA Ops:
  0.7 146.4 %shard_map.316 = (bf16[2,1,256,384]{3,2,1,0:T(8,128)(2,1)}, bf16[2,1,256,384]{3,2,1,0:T(8,128)(2,1)}, bf16[6,2,2,64,768]{4,3,2,1,0:T(8,128)(2,1)}, bf16[6,2,2,19...) custom-call(bf16[2,1,256,384]{3,2,1,0:T(8,128)(2,1)} %refs_0_.1, bf16[2,1,256,384]{3,2,1,0:T(8,128)(2,1)} %refs_1_.1, ...), custom_call_target="tpu_custom_call" | custom-call | tf_op jit(solution)/shard_map/pallas_call | solution.py:1085
  147.1 8.2 %shard_map.317 = (f32[1536,768]{1,0:T(8,128)}, f32[768,1536]{1,0:T(8,128)}, bf16[2,1,256,384]{3,2,1,0:T(8,128)(2,1)}, bf16[2,1,256,384]{3,2,1,0:T(8,128)(2,1)}, ...) custom-call(bf16[6,2,2,64,768]{4,3,2,1,0:T(8,128)(2,1)} %get-tuple-e, ...), custom_call_target="tpu_custom_call" | custom-call | tf_op jit(solution)/shard_map/pallas_call | solution.py:1132

commit v3 on v2

--- a/solution.py
+++ b/solution.py
@@ -73,8 +73,20 @@
 
 
 RANKS = 16
-STAGES = 8
-HIGH = lax.Precision.HIGH
+STAGES = 10
+CUTS = 2
+ASYNC = (
+    ("cotangent_in", "cotangent"),
+    ("log_step_in", "log_step"),
+    ("log_decay_in", "log_decay"),
+    ("frequency_in", "frequency"),
+    ("b_in_in", "b_in"),
+    ("c_out_in", "c_out"),
+    ("to_hi_in", "to_hi"),
+    ("to_lo_in", "to_lo"),
+    ("from_hi_in", "from_hi"),
+    ("from_lo_in", "from_lo"),
+)
 BF16 = jnp.bfloat16
 F32 = jnp.float32
 NT = (((1,), (1,)), ((), ()))
@@ -91,31 +103,55 @@
     from_re, from_im = cosine / length, -sine / length
     from_re[0] /= 2
     from_im[0] = sign / (2 * length)
-    return tuple(t.astype(np.float32) for t in (to_re, to_im, from_re, from_im))
+    tables = []
+    for table in (np.concatenate([to_re, to_im], 1), np.concatenate([from_re, from_im], 0)):
+        high = table.astype(BF16)
+        tables += [high, (table - high.astype(np.float64)).astype(BF16)]
+    return tuple(tables)
+
+
+def by_table(values, high, low):
+    def dot(a, b):
+        return jnp.dot(a, b[...], preferred_element_type=F32)
+
+    if values.dtype == BF16:
+        return dot(values, high) + dot(values, low)
+    first = values.astype(BF16)
+    second = (values - first.astype(F32)).astype(BF16)
+    return dot(first, high) + (dot(first, low) + dot(second, high))
 
 
 def times(a, b):
     return a[0] * b[0] - a[1] * b[1], a[0] * b[1] + a[1] * b[0]
 
 
-def reduce_stage(stage, c, role, places, keep, first, third, bufs):
+def up_cut(shape, q):
+    rows, cols = shape[0] * 2 // CUTS, shape[1] // 2
+    return (
+        slice(q // 2 * rows, (q // 2 + 1) * rows),
+        slice(q % 2 * cols, (q % 2 + 1) * cols),
+    )
+
+
+def reduce_stage(stage, c, role, places, lines, send, recv):
     near, inner, outer = places
     far = 1 - near
-    part, from_first, from_outer, from_inner, from_third, full, send, recv = bufs
-
-    def remote(src, dst, kind, target):
-        return pltpu.make_async_remote_copy(
+
+    def start(kind, src, dst, target):
+        pltpu.make_async_remote_copy(
             src_ref=src,
             dst_ref=dst,
-            send_sem=send.at[kind, c],
+            send_sem=send.at[kind],
             recv_sem=recv.at[kind, c],
             device_id=target,
             device_id_type=MESH,
-        )
-
-    def piece(which, kind, target):
-        place = full.at[c, keep, which]
-        return remote(place, place, kind, target)
+        ).start()
+
+    def landed(kind, ref):
+        pltpu.make_async_copy(ref, ref, recv.at[kind, c]).wait()
+
+    halves = lines[0].part.at[c]
+    quarters = lines[0].from_first.at[c]
 
     def added(*refs):
         total = refs[0][...].astype(F32)
@@ -123,106 +159,122 @@
             total = total + ref[...].astype(F32)
         return total.astype(BF16)
 
-    def to_first():
-        return remote(part.at[c, 1 - keep], from_first.at[c], 0, first)
-
-    def far_in():
-        return remote(part.at[c, keep, far], from_outer.at[c, 0], 1, inner)
-
-    def near_in():
-        return remote(part.at[c, keep, near], from_outer.at[c, 1], 2, inner)
-
-    def far_over():
-        return remote(part.at[c, keep, far], from_inner.at[c], 3, inner)
-
-    def to_third():
-        return remote(part.at[c, keep, near], from_third.at[c], 4, third)
-
-    def back(half):
-        return remote(full.at[c, half], full.at[c, half], 8, first)
+    def give(kind, which, target):
+        for line in lines:
+            place = line.full.at[c, line.keep, which]
+            start(kind, place, place, target)
+
+    def give_back():
+        for line in lines:
+            place = line.full.at[c, line.keep]
+            start(8, place, place, line.first)
 
     if stage == 0:
 
         @pl.when(role > 0)
         def _():
-            to_first().start()
+            for line in lines:
+                start(0, line.part.at[c, 1 - line.keep], line.from_first.at[c], line.first)
 
     elif stage == 1:
 
         @pl.when(role > 0)
         def _():
-            to_first().wait_recv()
-            part[c, keep] = added(part.at[c, keep], from_first.at[c])
+            landed(0, halves)
+            for line in lines:
+                line.part[c, line.keep] = added(line.part.at[c, line.keep], line.from_first.at[c])
 
         @pl.when(role == 1)
         def _():
-            far_in().start()
-            near_in().start()
+            for line in lines:
+                start(1, line.part.at[c, line.keep, far], line.from_outer.at[c], inner)
 
     elif stage == 2:
 
         @pl.when(role == 2)
         def _():
-            far_in().wait_recv()
-            part[c, keep, far] = added(part.at[c, keep, far], from_outer.at[c, 0])
-            far_over().start()
+            landed(1, quarters)
+            for line in lines:
+                mine = line.part.at[c, line.keep, far]
+                mine[...] = added(mine, line.from_outer.at[c])
+                start(2, mine, line.from_inner.at[c], inner)
 
     elif stage == 3:
 
         @pl.when(role == 2)
         def _():
-            near_in().wait_recv()
-            far_over().wait_recv()
-            part[c, keep, near] = added(
-                part.at[c, keep, near], from_outer.at[c, 1], from_inner.at[c]
-            )
-            to_third().start()
+            landed(2, quarters)
+            for line in lines:
+                mine = line.part.at[c, line.keep, near]
+                mine[...] = added(mine, line.from_inner.at[c])
+                start(3, mine, line.from_inner.at[c], outer)
 
     elif stage == 4:
+
+        @pl.when(role == 1)
+        def _():
+            landed(3, quarters)
+            for line in lines:
+                mine = line.part.at[c, line.keep, near]
+                mine[...] = added(mine, line.from_inner.at[c])
+                start(4, mine, line.from_third.at[c], line.third)
+
+    elif stage == 5:
+
+        @pl.when(role == 1)
+        def _():
+            landed(4, quarters)
+            for line in lines:
+                mine = line.part.at[c, line.keep, near]
+                line.full[c, line.keep, near] = added(mine, line.from_third.at[c])
+            give(5, near, inner)
+
+    elif stage == 6:
 
         @pl.when(role == 2)
         def _():
-            to_third().wait_recv()
-            full[c, keep, near] = added(part.at[c, keep, near], from_third.at[c])
-            piece(near, 5, outer).start()
-            piece(near, 6, inner).start()
-
-    elif stage == 5:
+            landed(5, quarters)
+            give(6, near, inner)
+
+    elif stage == 7:
 
         @pl.when(role == 2)
         def _():
-            piece(far, 6, inner).wait_recv()
-            piece(far, 7, outer).start()
-            back(keep).start()
-
-    elif stage == 6:
+            landed(6, quarters)
+            give(7, far, outer)
+            give_back()
+
+    elif stage == 8:
 
         @pl.when(role == 1)
         def _():
-            piece(near, 5, inner).wait_recv()
-            piece(far, 7, inner).wait_recv()
-            back(keep).start()
+            landed(7, quarters)
+            give_back()
 
     else:
 
         @pl.when(role > 0)
         def _():
-            back(1 - keep).wait_recv()
-            to_first().wait_send()
-            back(keep).wait_send()
-
-        @pl.when(role == 2)
-        def _():
-            far_over().wait_send()
-            to_third().wait_send()
-            piece(near, 5, outer).wait_send()
-            piece(near, 6, inner).wait_send()
-            piece(far, 7, outer).wait_send()
-
-        @pl.when(role == 1)
-        def _():
-            far_in().wait_send()
-            near_in().wait_send()
+            landed(8, halves)
+
+
+def reduce_sent(middle, lines, send):
+    halves, quarters = lines[0].part, lines[0].from_first
+
+    def gone(kinds):
+        for kind in kinds:
+            ref = halves if kind in (0, 8) else quarters
+            pltpu.make_async_copy(ref, ref, send.at[kind]).wait()
+
+    gone((0, 8))
+
+    @pl.when(middle == 0)
+    def _():
+        gone((1, 4, 5))
+
+    @pl.when(middle == 1)
+    def _():
+        gone((2, 3, 6, 7))
 
 
 def mode_values(modes):
@@ -271,6 +323,7 @@
     twin = (rank, 1 - core)
     heights, widths = v.heights, v.widths
     chunks, part = v.wd.shape[0], v.wd.shape[1]
+    pieces = CUTS * chunks
     slab, columns = v.rb1.shape[1:]
     own = slab // 2
     here = own * RANKS
@@ -298,28 +351,36 @@
     def wide(column):
         return jnp.concatenate([column] * (pixels // column.shape[1]), axis=1)
 
-    def scatter(sems, src, dst):
+    def partner(k):
+        return rank ^ lax.rem(7 * k, RANKS)
+
+    def slab_copy(sems, index, src, dst, d):
+        return pltpu.make_async_remote_copy(
+            src_ref=src,
+            dst_ref=dst,
+            send_sem=sems.at[0, 0],
+            recv_sem=sems.at[1, index],
+            device_id=(d, core),
+            device_id_type=MESH,
+        )
+
+    def scatter(sems, src, dst, each=False, first=1, count=RANKS - 1):
         def start(k):
-            d = lax.rem(rank + k, RANKS)
-            copy(src(d), dst, sems, k, (d, core)).start()
-
-        loop(RANKS, start, 1)
-
-    def arrived(sems, src, dst, then=None):
-        def wait(k):
-            s = lax.rem(rank + RANKS - k, RANKS)
-            copy(src(s), dst(s), sems, k, (s, core)).wait_recv()
-            if then is not None:
-                then(k, s)
-
-        loop(RANKS, wait, 1)
-
-    def scattered(sems, src, dst):
-        def wait(k):
-            d = lax.rem(rank + k, RANKS)
-            copy(src(d), dst, sems, k, (d, core)).wait_send()
-
-        loop(RANKS, wait, 1)
+            d = partner(k)
+
+            @pl.when(k < RANKS)
+            def _():
+                slab_copy(sems, k if each else 0, src.at[d], dst, d).start()
+
+        loop(first + count, start, first)
+
+    def all_slabs(sems, which, ref):
+        most = ref.at[pl.ds(0, RANKS - 1)]
+        pltpu.make_async_copy(most, most, sems.at[which, 0]).wait()
+
+    def bring(which):
+        far_ref, near_ref = ASYNC[which]
+        return pltpu.make_async_copy(getattr(v, far_ref), getattr(v, near_ref), v.bring.at[which])
 
     barrier = pltpu.get_barrier_semaphore()
 
@@ -333,17 +394,16 @@
 
     def fetch_up(m):
         cols = pl.ds(pl.multiple_of(m * part, part), part)
-        return pltpu.make_async_copy(v.w_up.at[:, cols], v.wu.at[m], v.fetch.at[0, m])
+        return pltpu.make_async_copy(v.w_up.at[:, cols], v.wu.at[m], v.fetch.at[0])
 
     def fetch_down(m):
         rows = pl.ds(pl.multiple_of(m * part, part), part)
-        return pltpu.make_async_copy(v.w_down.at[rows], v.wd.at[m], v.fetch.at[1, m])
+        return pltpu.make_async_copy(v.w_down.at[rows], v.wd.at[m], v.fetch.at[1])
 
     def fetch(m):
         fetch_up(m).start()
         fetch_down(m).start()
 
-    loop(chunks, fetch)
 
     for g in range(2):
         v.tok[:, g * columns : (g + 1) * columns] = v.tokens[g, 0].astype(F32).T
@@ -361,8 +421,11 @@
     lines.append(jnp.zeros((32 - len(lines), 128), F32))
     v.vx[core] = jnp.concatenate(lines, axis=0)
     pl.semaphore_wait(barrier, RANKS)
-    scatter(v.a1, lambda d: v.tb.at[core, d], v.rb1.at[rank])
+    scatter(v.a1, v.tb.at[core], v.rb1.at[rank])
     v.rb1[rank] = v.tb[core, rank]
+    for which in range(len(ASYNC)):
+        bring(which).start()
+    loop(chunks, fetch)
     copy(v.tb.at[core], v.tb.at[core], v.tw, 0, twin).start()
     copy(v.vx.at[core], v.vx.at[core], v.tw, 1, twin).start()
 
@@ -381,6 +444,8 @@
             v.bias[m, q * 128 : (q + 1) * 128, :] = jnp.broadcast_to(
                 cols[:, 2 * m + q : 2 * m + q + 1], (128, 128)
             )
+    for which in range(len(ASYNC)):
+        bring(which).wait()
     for g in range(2):
         v.cot[:, g * columns : (g + 1) * columns] = v.cotangent[g, 0].astype(F32).T
     places_w = lax.broadcasted_iota(jnp.int32, (1, columns), 1)
@@ -447,8 +512,8 @@
     k_width = lax.dot_general(
         v.pick[...], v.kt[...], NT, precision=PRECISE, preferred_element_type=F32
     )
-    k_re = jnp.dot(k_width, v.to_re[...], precision=PRECISE, preferred_element_type=F32)
-    k_im = jnp.dot(k_width, v.to_im[...], precision=PRECISE, preferred_element_type=F32)
+    k_both = by_table(k_width, v.to_hi, v.to_lo)
+    k_re, k_im = k_both[:, :columns], k_both[:, columns:]
     first_lane = lax.broadcasted_iota(jnp.int32, (slab, columns), 1) == 0
     v.ks[0] = k_re
     v.ks[1] = jnp.where(first_lane, 0.0, k_im)
@@ -456,37 +521,36 @@
     coef_h = tuple(2.0 * part_of[0:1] for part_of in mv.coef)
     v.kt[0:RANKS, :] = coef_h[0] * v.eh[0] - coef_h[1] * v.eh[1]
 
-    def k_height(l):
-        taps = jnp.sum(v.pick[...] * v.kt[pl.ds(l, 1), :], axis=1, keepdims=True)
-        v.kh[l] = jnp.broadcast_to(taps, (slab, 128))
-
-    loop(RANKS, k_height)
+    taps = lax.dot_general(
+        v.pick[...], v.kt[0:RANKS, :], NT, precision=PRECISE, preferred_element_type=F32
+    )
+    for l in range(RANKS):
+        v.kh[l] = jnp.broadcast_to(taps[:, l : l + 1], (slab, 128))
+
+    pltpu.make_async_copy(v.wu, v.wu, v.fetch.at[0]).wait()
+    pltpu.make_async_copy(v.wd, v.wd, v.fetch.at[1]).wait()
 
     def turn(m):
-        fetch_up(m).wait()
-        fetch_down(m).wait()
         v.wut[m] = v.wu[m].T
         v.wdt[m] = v.wd[m].T
 
     loop(chunks // 2, turn)
 
-    arrived(v.a1, lambda s: v.tb.at[core, s], lambda s: v.rb1.at[s])
+    all_slabs(v.a1, 1, v.rb1)
     step_rows = 4
 
     def convolve(b):
         at = pl.ds(b * step_rows, step_rows)
-        values = v.rb1[at].reshape(step_rows * slab, columns).astype(F32)
+        values = v.rb1[at].reshape(step_rows * slab, columns)
         shape = (step_rows, slab, columns)
-        x_re = jnp.dot(values, v.to_re[...], precision=HIGH, preferred_element_type=F32)
-        x_im = jnp.dot(values, v.to_im[...], precision=HIGH, preferred_element_type=F32)
-        x_re, x_im = x_re.reshape(shape), x_im.reshape(shape)
+        x_both = by_table(values, v.to_hi, v.to_lo)
+        x_re, x_im = x_both[:, :columns].reshape(shape), x_both[:, columns:].reshape(shape)
         v.xs[0, at] = x_re
         v.xs[1, at] = x_im
         k0, k1, k2 = v.ks[0], v.ks[1], v.ks[2]
-        y_re = (x_re * k0 - x_im * k1).reshape(step_rows * slab, columns)
-        y_im = (x_re * k1 + x_im * k2).reshape(step_rows * slab, columns)
-        along = jnp.dot(y_re, v.from_re[...], precision=HIGH, preferred_element_type=F32)
-        along += jnp.dot(y_im, v.from_im[...], precision=HIGH, preferred_element_type=F32)
+        y_both = jnp.concatenate([x_re * k0 - x_im * k1, x_re * k1 + x_im * k2], axis=2)
+        y_both = y_both.reshape(step_rows * slab, 2 * columns)
+        along = by_table(y_both, v.from_hi, v.from_lo)
         v.along[at] = along.astype(BF16).astype(F32).reshape(shape)
 
     loop(RANKS // step_rows, convolve)
@@ -509,7 +573,7 @@
 
     by_tiles(down_rows)
     v.sb2[...] = v.tall[...].astype(BF16)
-    scatter(v.a2, lambda d: v.sb2.at[d], v.rb2.at[core, rank])
+    scatter(v.a2, v.sb2, v.rb2.at[core, rank], each=True)
     v.rb2[core, rank] = v.sb2[rank]
     copy(v.rb2.at[core, rank], v.rb2.at[core, rank], v.fw, 0, twin).start()
 
@@ -519,17 +583,14 @@
     v.branch[...] = jnp.zeros_like(v.branch)
     v.gn[...] = jnp.zeros_like(v.gn)
 
-    def forward(k, s):
-        copy(v.rb2.at[core, s], v.rb2.at[core, s], v.fw, k, twin).start()
-
-    arrived(v.a2, lambda s: v.sb2.at[s], lambda s: v.rb2.at[core, s], forward)
+    def forward(k):
+        d = partner(k)
+        slab_copy(v.a2, k, v.sb2.at[d], v.rb2.at[core, d], d).wait_recv()
+        copy(v.rb2.at[core, d], v.rb2.at[core, d], v.fw, 0, twin).start()
+
+    loop(RANKS, forward, 1)
     copy(v.tb.at[core], v.tb.at[1 - core], v.tw, 0, twin).wait_recv()
-
-    def forwarded(k):
-        s = lax.rem(rank + RANKS - k, RANKS)
-        copy(v.rb2.at[core, s], v.rb2.at[1 - core, s], v.fw, k, twin).wait_recv()
-
-    loop(RANKS, forwarded)
+    copy(v.rb2.at[core], v.rb2.at[1 - core], v.fw, 0, twin).wait_recv()
 
     eight = jnp.zeros((8, pixels), F32)
 
@@ -586,9 +647,12 @@
         g_active = jnp.dot(v.wd[t], g_branch, preferred_element_type=F32)
         g_hidden = (g_active * slope).astype(BF16)
         down = lax.dot_general(active, g_branch, NT, preferred_element_type=F32)
-        v.pd[t] = down.astype(BF16).reshape(2, 2, part // 4, channels)
+        down = down.astype(BF16).reshape(CUTS, 2, 2, part // CUTS // 4, channels)
+        v.pd[pl.ds(CUTS * t, CUTS)] = down
         up = lax.dot_general(normed, g_hidden, NT, preferred_element_type=F32)
-        v.pu[t] = up.astype(BF16).reshape(2, 2, channels // 4, part)
+        up = up.astype(BF16)
+        for q in range(CUTS):
+            v.pu[CUTS * t + q] = up[up_cut(up.shape, q)].reshape(v.pu.shape[1:])
         v.gn[...] += jnp.dot(v.wu[t], g_hidden, preferred_element_type=F32)
         v.branch[...] += jnp.dot(v.wdt[t], active, preferred_element_type=F32)
         ones = jnp.ones((8, pixels), BF16)
@@ -639,7 +703,6 @@
             v.sb3[d] = both.astype(BF16)
 
         loop(RANKS, each)
-        scatter(v.a3, lambda d: v.sb3.at[d], v.rb3.at[rank])
         v.rb3[rank] = v.sb3[rank]
 
     def outputs():
@@ -657,10 +720,11 @@
 
         loop(here // 128, rows)
         for g in range(2):
-            v.output[g, 0] = v.res[:, g * columns : (g + 1) * columns].T.astype(BF16)
+            v.o_out[g, 0] = v.res[:, g * columns : (g + 1) * columns].T.astype(BF16)
+        pltpu.make_async_copy(v.o_out, v.output, v.leave.at[2]).start()
 
     def convolve_back():
-        arrived(v.a3, lambda s: v.sb3.at[s], lambda s: v.rb3.at[s])
+        all_slabs(v.a3, 1, v.rb3)
         v.tall[...] = v.rb3[...].astype(F32)
 
         def up_rows(at, cut):
@@ -689,16 +753,14 @@
         def one_step(b, totals):
             at = pl.ds(b * step_rows, step_rows)
             shape = (step_rows, slab, columns)
-            values = v.galong[at].reshape(step_rows * slab, columns)
-            g_re = jnp.dot(values, v.to_re[...], precision=HIGH, preferred_element_type=F32)
-            g_im = jnp.dot(values, v.to_im[...], precision=HIGH, preferred_element_type=F32)
-            g_re, g_im = g_re.reshape(shape), g_im.reshape(shape)
+            values = v.galong[at].reshape(step_rows * slab, columns).astype(BF16)
+            g_both = by_table(values, v.to_hi, v.to_lo)
+            g_re, g_im = g_both[:, :columns].reshape(shape), g_both[:, columns:].reshape(shape)
             x_re, x_im = v.xs[0, at], v.xs[1, at]
             k0, k1, k2 = v.ks[0], v.ks[1], v.ks[2]
-            y_re = (g_re * k0 + g_im * k1).reshape(step_rows * slab, columns)
-            y_im = (g_im * k2 - g_re * k1).reshape(step_rows * slab, columns)
-            conv = jnp.dot(y_re, v.from_re[...], precision=HIGH, preferred_element_type=F32)
-            conv += jnp.dot(y_im, v.from_im[...], precision=HIGH, preferred_element_type=F32)
+            y_both = jnp.concatenate([g_re * k0 + g_im * k1, g_im * k2 - g_re * k1], axis=2)
+            y_both = y_both.reshape(step_rows * slab, 2 * columns)
+            conv = by_table(y_both, v.from_hi, v.from_lo)
             v.sb4[at] = conv.reshape(shape).astype(BF16)
             return (
                 totals[0] + (x_re * g_re).sum(axis=0),
@@ -707,23 +769,30 @@
             )
 
         cross = lax.fori_loop(0, RANKS // step_rows, one_step, (none, none, none))
-        scatter(v.a4, lambda d: v.sb4.at[d], v.rb4.at[rank])
         v.rb4[rank] = v.sb4[rank]
+        for q in range(3):
+            v.cross[q] = cross[q]
+
+    def kernel_grads():
+        cross = [v.cross[q] for q in range(3)]
         zero_lane = lax.broadcasted_iota(jnp.int32, (slab, columns), 1) == 0
         c_re = cross[0] + jnp.where(zero_lane, 0.0, cross[1])
         c_im = jnp.where(zero_lane, cross[1], cross[2])
-        dk_width = jnp.dot(c_re, v.from_re[...], precision=PRECISE, preferred_element_type=F32)
-        dk_width += jnp.dot(c_im, v.from_im[...], precision=PRECISE, preferred_element_type=F32)
+        dk_width = by_table(jnp.concatenate([c_re, c_im], axis=1), v.from_hi, v.from_lo)
         v.kt[...] = lax.dot_general(
             dk_width, v.pick[...], TN, precision=PRECISE, preferred_element_type=F32
         )
 
-        def lag_height(l):
-            at = pl.ds(l, 1)
-            lag = jnp.sum(v.lags[l], axis=1, keepdims=True)
-            v.kth[at, :] = jnp.sum(lag * v.pick[...], axis=0, keepdims=True)
-
-        loop(RANKS, lag_height)
+        lags = v.lags[...].reshape(RANKS * slab, columns)
+        first = lags.astype(BF16)
+        second = (lags - first.astype(F32)).astype(BF16)
+        ones = jnp.ones((columns, 128), BF16)
+        lags = jnp.dot(first, ones, preferred_element_type=F32)
+        lags += jnp.dot(second, ones, preferred_element_type=F32)
+        lags = lags.reshape(RANKS, slab, 128)
+        for q in range(lanes // 128):
+            cut = slice(q * 128, (q + 1) * 128)
+            v.kth[:, cut] = jnp.sum(lags * v.pick[:, cut][None], axis=1)
         parameters()
 
     def parameters():
@@ -809,7 +878,7 @@
         copy(mine, mine, v.ga, 5, beside).start()
 
     def token_grads():
-        arrived(v.a4, lambda s: v.sb4.at[s], lambda s: v.rb4.at[s])
+        all_slabs(v.a4, 1, v.rb4)
 
         def rows(d):
             at = pl.ds(pl.multiple_of(d * own, 8), own)
@@ -820,74 +889,113 @@
 
         loop(RANKS, rows)
         for g in range(2):
-            v.d_tokens[g, 0] = v.res[:, g * columns : (g + 1) * columns].T.astype(BF16)
-
-    down = (v.pd, v.d1, v.d2, v.d3, v.d4, v.fd, v.d_sems.at[0], v.d_sems.at[1])
-    up = (v.pu, v.u1, v.u2, v.u3, v.u4, v.fu, v.u_sems.at[0], v.u_sems.at[1])
+            v.t_out[g, 0] = v.res[:, g * columns : (g + 1) * columns].T.astype(BF16)
+        pltpu.make_async_copy(v.t_out, v.d_tokens, v.leave.at[3]).start()
+
+    down = types.SimpleNamespace(
+        part=v.pd,
+        from_first=v.d1,
+        from_outer=v.d2,
+        from_inner=v.d3,
+        from_third=v.d4,
+        full=v.fd,
+        keep=x,
+        first=beside,
+        third=across,
+    )
+    up = types.SimpleNamespace(
+        part=v.pu,
+        from_first=v.u1,
+        from_outer=v.u2,
+        from_inner=v.u3,
+        from_third=v.u4,
+        full=v.fu,
+        keep=y,
+        first=across,
+        third=beside,
+    )
 
     def leave(c):
         return (
-            pltpu.make_async_copy(v.fd.at[c], v.down.at[c], v.leave.at[0, c]),
-            pltpu.make_async_copy(v.fu.at[c], v.up.at[c], v.leave.at[1, c]),
+            pltpu.make_async_copy(v.fd.at[c], v.down.at[c], v.leave.at[0]),
+            pltpu.make_async_copy(v.fu.at[c], v.up.at[c], v.leave.at[1]),
         )
 
+
+    def advance(stage, c, role):
+        reduce_stage(stage, c, role, places, (down, up), v.sent, v.landed)
+
+    def known(stage, c):
+        live = (c * (pieces - 1 - c) >= 0).astype(jnp.int32)
+        advance(stage, c, live * (1 + middle))
+        if stage == STAGES - 1:
+
+            @pl.when(live > 0)
+            def _():
+                for one in leave(c):
+                    one.start()
+
     events = {
-        chunks: norm_back,
-        chunks + 1: outputs,
-        chunks + 3: convolve_back,
-        chunks + 4: gather_across,
-        chunks + 5: gather_beside,
-        chunks + 6: token_grads,
+        0: norm_back,
+        3: outputs,
+        9: convolve_back,
+        11: kernel_grads,
+        13: gather_across,
+        15: gather_beside,
+        21: token_grads,
     }
 
+    def feed_and_send(t):
+        feed(t)
+        for q in range(CUTS):
+            c = CUTS * t + q
+            advance(0, c, (c < 4).astype(jnp.int32) * (1 + middle))
+
+    loop(chunks, feed_and_send)
+    share()
+
     def tick(t, carry):
-        @pl.when(t < chunks)
-        def _():
-            feed(t)
-
-        pl.when(t == chunks - 1)(share)
         for when, event in events.items():
             pl.when(t == when)(event)
-        for stage in range(STAGES - 1, -1, -1):
-            c = t - stage
-            live = (c * (chunks - 1 - c) >= 0).astype(jnp.int32)
-            role = live * (1 + middle)
-            reduce_stage(stage, c, role, places, x, beside, across, down)
-            reduce_stage(stage, c, role, places, y, across, beside, up)
-            if stage == STAGES - 1:
-
-                @pl.when(live > 0)
-                def _():
-                    for one in leave(c):
-                        one.start()
-
+        for when, sems, src, dst in (
+            (0, v.a3, v.sb3, v.rb3),
+            (9, v.a4, v.sb4, v.rb4),
+        ):
+            batch = t - when
+
+            @pl.when(batch * (8 - 1 - batch) >= 0)
+            def _():
+                scatter(sems, src, dst.at[rank], first=1 + 2 * batch, count=2)
+
+        for q in range(1):
+            c = 4 + 1 * (t - 0) + q
+            known(0, jnp.where(t < 0, pieces, c))
+        for stage, start in enumerate((0,2,4,6,8,10,12,14,16), 1):
+            for q in range(1):
+                known(stage, 1 * (t - start) + q)
         return carry
 
-    lax.fori_loop(0, chunks + STAGES - 1, tick, 0)
+    lax.fori_loop(0, pieces // 1 + (0,2,4,6,8,10,12,14,16)[-1], tick, 0)
 
     theirs = v.gathered.at[:, :, 1 - x]
     copy(theirs, theirs, v.ga, 5, beside).wait_recv()
 
-    def left(c):
-        for one in leave(c):
-            one.wait()
-
-    loop(chunks, left)
-    scattered(v.a1, lambda d: v.tb.at[core, d], v.rb1.at[rank])
-    scattered(v.a2, lambda d: v.sb2.at[d], v.rb2.at[core, rank])
-    scattered(v.a3, lambda d: v.sb3.at[d], v.rb3.at[rank])
-    scattered(v.a4, lambda d: v.sb4.at[d], v.rb4.at[rank])
+    pltpu.make_async_copy(v.fd, v.down, v.leave.at[0]).wait()
+    pltpu.make_async_copy(v.fu, v.up, v.leave.at[1]).wait()
+    pltpu.make_async_copy(v.o_out, v.output, v.leave.at[2]).wait()
+    pltpu.make_async_copy(v.t_out, v.d_tokens, v.leave.at[3]).wait()
+    all_slabs(v.a1, 0, v.rb1)
+    all_slabs(v.a2, 0, v.sb2)
+    all_slabs(v.a3, 0, v.sb3)
+    all_slabs(v.a4, 0, v.sb4)
+    reduce_sent(middle, (down, up), v.sent)
     copy(v.tb.at[core], v.tb.at[core], v.tw, 0, twin).wait_send()
     copy(v.vx.at[core], v.vx.at[core], v.tw, 1, twin).wait_send()
     copy(v.gb.at[core], v.gb.at[core], v.tw, 2, twin).wait_send()
     copy(v.gn_out, v.gn_in, v.tw, 3, twin).wait_send()
     copy(v.br_out, v.br_in, v.tw, 4, twin).wait_send()
 
-    def forward_sent(k):
-        s = lax.rem(rank + RANKS - k, RANKS)
-        copy(v.rb2.at[core, s], v.rb2.at[core, s], v.fw, k, twin).wait_send()
-
-    loop(RANKS, forward_sent)
+    copy(v.rb2.at[core], v.rb2.at[core], v.fw, 0, twin).wait_send()
 
     def gather_sent(k):
         target = (lax.rem(z + k, 4) * 4 + y * 2 + x, core)
@@ -900,47 +1008,101 @@
     copy(mine, mine, v.ga, 5, beside).wait_send()
 
 
-def finish_kernel(own, down, up, gathered, output, d_tokens, *outs):
-    d_w_down, d_w_up, output_out, d_tokens_out = outs[:4]
-    d_log_step, d_log_decay, d_frequency, d_b_in, d_c_out = outs[4:9]
-    d_w_down[...] = down[...].reshape(d_w_down.shape).astype(F32)
-    d_w_up[...] = up[...].reshape(d_w_up.shape).astype(F32)
+def finish_kernel(own, *refs):
+    ins, outs, small, near, wide, sems = refs[:5], refs[5:20], refs[20:33], refs[33:36], refs[36:38], refs[38:]
+    brought, moved, left = sems
+    pieces, rows = near[0].shape[0], wide[0].shape[1]
+    group = pieces // brought.shape[1]
+
+    def bring(which, m):
+        some = pl.ds(m * group, group)
+        return pltpu.make_async_copy(
+            ins[which].at[some], near[which].at[some], brought.at[which, m]
+        )
+
+    def leave(which, m):
+        if which == 0:
+            place = outs[0].at[pl.ds(pl.multiple_of(m * rows, rows), rows)]
+        else:
+            up_rows, up_cols = wide[1].shape[1:]
+            place = outs[1].at[
+                pl.ds(pl.multiple_of(m % CUTS // 2 * up_rows, 16), up_rows),
+                pl.ds(pl.multiple_of((m // CUTS * 2 + m % 2) * up_cols, 128), up_cols),
+            ]
+        return pltpu.make_async_copy(wide[which].at[m], place, left.at[which])
+
+    brings = [
+        pltpu.make_async_copy(src, dst, brought.at[2, k])
+        for k, (src, dst) in enumerate(zip(ins[2:], (near[2],) + small[:2]))
+    ]
+    moves = [
+        pltpu.make_async_copy(src, dst, moved.at[k])
+        for k, (src, dst) in enumerate(zip(small, outs[2:]))
+    ]
+
+    def each(count, body):
+        def step(m, carry):
+            for which in range(2):
+                body(which, m)
+            return carry
+
+        lax.fori_loop(0, count, step, 0)
+
+    def widen(which, m):
+        bring(which, m).wait()
+        for q in range(group):
+            one = group * m + q
+            wide[which][one] = near[which][one].reshape(wide[which].shape[1:]).astype(F32)
+            leave(which, one).start()
+
+    for one in brings:
+        one.start()
+    each(brought.shape[1], lambda which, m: bring(which, m).start())
+    for one in brings:
+        one.wait()
+    widen_small(own, near[2], small[2:])
+    for one in moves:
+        one.start()
+    each(brought.shape[1], widen)
+    for which in range(2):
+        pltpu.make_async_copy(wide[which], wide[which], left.at[which]).wait()
+    for one in moves:
+        one.wait()
+
+
+def widen_small(own, gathered, small):
+    d_log_step, d_log_decay, d_frequency, d_b_in, d_c_out = small[:5]
     per, here = d_log_decay.shape[1:]
-
-    @pl.when(pl.program_id(0) == 0)
-    def _():
-        output_out[...] = output[...]
-        d_tokens_out[...] = d_tokens[...]
-        lane = lax.broadcasted_iota(jnp.int32, (per, 128), 1)
-        whole = []
-        for r in range(14):
-            five, k = divmod(r, 5)
-            windows = [jnp.zeros((per, 128), F32) for _ in range(here // 128)]
-            for s in range(RANKS):
-                block = gathered[s // 4, s // 2 % 2, s % 2, five * per : (five + 1) * per, :]
-                turned = pltpu.roll(block.astype(F32), (own * (s - k)) % 128, 1)
-                window, low = divmod(own * s, 128)
-                inside = (lane >= low) & (lane < low + own)
-                windows[window] = jnp.where(inside, turned, windows[window])
-                if low + own > 128:
-                    inside = lane < low + own - 128
-                    windows[window + 1] = jnp.where(inside, turned, windows[window + 1])
-            whole.append(jnp.concatenate(windows, axis=1))
-        for a in range(2):
-            d_log_step[a : a + 1, :] = jnp.sum(whole[a], axis=0, keepdims=True)
-            d_log_decay[a] = whole[2 + a]
-            d_frequency[a] = whole[4 + a]
-            for i in range(2):
-                d_b_in[a, i] = whole[6 + 2 * i + a]
-                d_c_out[a, i] = whole[10 + 2 * i + a]
-        sums = jnp.zeros((32, 128), F32)
+    lane = lax.broadcasted_iota(jnp.int32, (per, 128), 1)
+    whole = []
+    for r in range(14):
+        five, k = divmod(r, 5)
+        windows = [jnp.zeros((per, 128), F32) for _ in range(here // 128)]
         for s in range(RANKS):
-            sums += gathered[s // 4, s // 2 % 2, s % 2, 3 * per :, :].astype(F32)
-        row = 0
-        for vector in outs[9:]:
-            for q in range(vector.shape[0] // 128):
-                vector[pl.ds(q * 128, 128)] = sums[row]
-                row += 1
+            block = gathered[s // 4, s // 2 % 2, s % 2, five * per : (five + 1) * per, :]
+            turned = pltpu.roll(block.astype(F32), (own * (s - k)) % 128, 1)
+            window, low = divmod(own * s, 128)
+            inside = (lane >= low) & (lane < low + own)
+            windows[window] = jnp.where(inside, turned, windows[window])
+            if low + own > 128:
+                inside = lane < low + own - 128
+                windows[window + 1] = jnp.where(inside, turned, windows[window + 1])
+        whole.append(jnp.concatenate(windows, axis=1))
+    for a in range(2):
+        d_log_step[a : a + 1, :] = jnp.sum(whole[a], axis=0, keepdims=True)
+        d_log_decay[a] = whole[2 + a]
+        d_frequency[a] = whole[4 + a]
+        for i in range(2):
+            d_b_in[a, i] = whole[6 + 2 * i + a]
+            d_c_out[a, i] = whole[10 + 2 * i + a]
+    sums = jnp.zeros((32, 128), F32)
+    for s in range(RANKS):
+        sums += gathered[s // 4, s // 2 % 2, s % 2, 3 * per :, :].astype(F32)
+    row = 0
+    for vector in small[5:]:
+        for q in range(vector.shape[0] // 128):
+            vector[pl.ds(q * 128, 128)] = sums[row]
+            row += 1
 
 
 def block_shards(
@@ -979,14 +1141,14 @@
     anywhere = pl.BlockSpec(memory_space=pl.ANY)
     inputs = dict(
         tokens=(tokens, in_vmem),
-        cotangent=(cotangent, in_vmem),
+        cotangent_in=(cotangent, anywhere),
         heights=(heights, in_smem),
         widths=(widths, in_smem),
-        log_step=(log_step, in_vmem),
-        log_decay=(log_decay.swapaxes(-1, -2), in_vmem),
-        frequency=(frequency.swapaxes(-1, -2), in_vmem),
-        b_in=(b_in.swapaxes(-1, -2), in_vmem),
-        c_out=(c_out.swapaxes(-1, -2), in_vmem),
+        log_step_in=(log_step, anywhere),
+        log_decay_in=(log_decay.swapaxes(-1, -2), anywhere),
+        frequency_in=(frequency.swapaxes(-1, -2), anywhere),
+        b_in_in=(b_in.swapaxes(-1, -2), anywhere),
+        c_out_in=(c_out.swapaxes(-1, -2), anywhere),
         b_up=(b_up, in_vmem),
         skip_gain=(skip_gain, in_vmem),
         ln_gain=(ln_gain, in_vmem),
@@ -995,16 +1157,16 @@
         b_down=(b_down, in_vmem),
         w_up=(w_up, anywhere),
         w_down=(w_down, anywhere),
-        to_re=(tables[0], in_vmem),
-        to_im=(tables[1], in_vmem),
-        from_re=(tables[2], in_vmem),
-        from_im=(tables[3], in_vmem),
-    )
-    down_shape = (chunks, 2, 2, part // 4, channels)
-    up_shape = (chunks, 2, 2, channels // 4, part)
+        to_hi_in=(tables[0], anywhere),
+        to_lo_in=(tables[1], anywhere),
+        from_hi_in=(tables[2], anywhere),
+        from_lo_in=(tables[3], anywhere),
+    )
+    down_shape = (CUTS * chunks, 2, 2, part // CUTS // 4, channels)
+    up_shape = (CUTS * chunks, 2, 2, channels // (2 * CUTS), part // 2)
     outs = dict(
-        output=(jax.ShapeDtypeStruct(tokens.shape, BF16), in_vmem),
-        d_tokens=(jax.ShapeDtypeStruct(tokens.shape, BF16), in_vmem),
+        output=(jax.ShapeDtypeStruct(tokens.shape, BF16), anywhere),
+        d_tokens=(jax.ShapeDtypeStruct(tokens.shape, BF16), anywhere),
         down=(jax.ShapeDtypeStruct(down_shape, BF16), anywhere),
         up=(jax.ShapeDtypeStruct(up_shape, BF16), anywhere),
         gathered=(jax.ShapeDtypeStruct((4, 2, 2, 3 * modes_each + 32, 128), BF16), in_vmem),
@@ -1036,6 +1198,7 @@
         gb=pltpu.VMEM((2, here, pixels), BF16),
         modes=pltpu.VMEM((16, lanes), F32),
         of_mode=pltpu.VMEM((modes_each, lanes), F32),
+        cross=pltpu.VMEM((3, 2 * own, columns), F32),
         pick=pltpu.VMEM((2 * own, lanes), F32),
         eh=pltpu.VMEM((2, RANKS, lanes), F32),
         ej=pltpu.VMEM((2, columns // 8, lanes), F32),
@@ -1060,8 +1223,21 @@
         dbu=pltpu.VMEM((chunks, 8, part), F32),
         sums=pltpu.VMEM((5, here, 128), F32),
         pack=pltpu.VMEM((3 * modes_each + 32, 128), BF16),
-        fetch=pltpu.SemaphoreType.DMA((2, chunks)),
-        leave=pltpu.SemaphoreType.DMA((2, chunks)),
+        fetch=pltpu.SemaphoreType.DMA((2,)),
+        leave=pltpu.SemaphoreType.DMA((4,)),
+        bring=pltpu.SemaphoreType.DMA((len(ASYNC),)),
+        o_out=pltpu.VMEM(tokens.shape, BF16),
+        t_out=pltpu.VMEM(tokens.shape, BF16),
+        cotangent=pltpu.VMEM(cotangent.shape, BF16),
+        log_step=pltpu.VMEM(log_step.shape, F32),
+        log_decay=pltpu.VMEM((2, modes_each, here), F32),
+        frequency=pltpu.VMEM((2, modes_each, here), F32),
+        b_in=pltpu.VMEM((2, 2, modes_each, here), F32),
+        c_out=pltpu.VMEM((2, 2, modes_each, here), F32),
+        to_hi=pltpu.VMEM(tables[0].shape, BF16),
+        to_lo=pltpu.VMEM(tables[1].shape, BF16),
+        from_hi=pltpu.VMEM(tables[2].shape, BF16),
+        from_lo=pltpu.VMEM(tables[3].shape, BF16),
     )
 
     def reduction(shape):
@@ -1069,17 +1245,20 @@
         whole = pltpu.VMEM(shape, BF16)
         half = pltpu.VMEM((count, pieces, rows, width), BF16)
         piece = pltpu.VMEM((count, rows, width), BF16)
-        return whole, half, half, piece, piece, whole, pltpu.SemaphoreType.DMA((2, 9, count))
+        return whole, half, piece, piece, piece, whole
 
     down_scratch, up_scratch = reduction(down_shape), reduction(up_shape)
     scratch.update(
-        zip(("pd", "d1", "d2", "d3", "d4", "fd", "d_sems"), down_scratch),
+        zip(("pd", "d1", "d2", "d3", "d4", "fd"), down_scratch),
     )
     scratch.update(
-        zip(("pu", "u1", "u2", "u3", "u4", "fu", "u_sems"), up_scratch),
-    )
-    several = pltpu.SemaphoreType.DMA((2, RANKS))
-    scratch.update(a1=several, a2=several, a3=several, a4=several, fw=several)
+        zip(("pu", "u1", "u2", "u3", "u4", "fu"), up_scratch),
+    )
+    one_each = pltpu.SemaphoreType.DMA((2, 1))
+    scratch.update(a1=one_each, a3=one_each, a4=one_each, fw=one_each)
+    scratch.update(a2=pltpu.SemaphoreType.DMA((2, RANKS)))
+    scratch.update(sent=pltpu.SemaphoreType.DMA((9,)))
+    scratch.update(landed=pltpu.SemaphoreType.DMA((9, CUTS * chunks)))
     scratch.update(tw=pltpu.SemaphoreType.DMA((2, 5)), ga=pltpu.SemaphoreType.DMA((2, 6)))
     names = tuple(inputs) + tuple(outs) + tuple(scratch)
     output, d_tokens, down, up, gathered = pl.pallas_call(
@@ -1092,9 +1271,6 @@
             collective_id=0, has_side_effects=True, vmem_limit_bytes=62 << 20
         ),
     )(*(value for value, _ in inputs.values()))
-    def fixed(shape):
-        return pl.BlockSpec(shape, lambda m, rank=len(shape): (0,) * rank)
-
     result = (
         jax.ShapeDtypeStruct((hidden, channels), F32),
         jax.ShapeDtypeStruct((channels, hidden), F32),
@@ -1131,20 +1307,18 @@
         d_layer_scale,
     ) = pl.pallas_call(
         functools.partial(finish_kernel, own),
-        grid=(chunks,),
         out_shape=result,
-        in_specs=[
-            pl.BlockSpec((1,) + down_shape[1:], lambda m: (m, 0, 0, 0, 0)),
-            pl.BlockSpec((1,) + up_shape[1:], lambda m: (m, 0, 0, 0, 0)),
-            fixed(gathered.shape),
-            fixed(tokens.shape),
-            fixed(tokens.shape),
+        in_specs=[anywhere] * 5,
+        out_specs=(anywhere,) * 15,
+        scratch_shapes=[pltpu.VMEM(one.shape, one.dtype) for one in result[2:]]
+        + [pltpu.VMEM(one.shape, BF16) for one in (down, up, gathered)]
+        + [
+            pltpu.VMEM((CUTS * chunks, part // CUTS, channels), F32),
+            pltpu.VMEM((CUTS * chunks, channels * 2 // CUTS, part // 2), F32),
+            pltpu.SemaphoreType.DMA((3, chunks)),
+            pltpu.SemaphoreType.DMA((13,)),
+            pltpu.SemaphoreType.DMA((2,)),
         ],
-        out_specs=(
-            pl.BlockSpec((part, channels), lambda m: (m, 0)),
-            pl.BlockSpec((channels, part), lambda m: (0, m)),
-        )
-        + tuple(fixed(one.shape) for one in result[2:]),
         compiler_params=pltpu.CompilerParams(vmem_limit_bytes=62 << 20),
     )(down, up, gathered, output, d_tokens)
     return (

time: 156 us -> 138 us (0.88)
  Pallas kernels: 155 us -> 137 us
    pallas_call x1, Pallas kernels: 146 us -> 131 us  [block_shards(): pl.pallas_call(functools.partial(block_kernel, names), out_shape=tuple((s...]
    pallas_call x1, Pallas kernels: 8.22 us -> 5.76 us  [block_shards(): pl.pallas_call(functools.partial(finish_kernel, own), out_shape=result, i...]
where the time goes in v3:
time: 138 us
  Pallas kernels  137 us (99%)
    pallas_call x1, Pallas kernels, block_shards(): pl.pallas_call(functools.partial(block_kernel, names), out_shape=tuple((s...  131 us
    pallas_call x1, Pallas kernels, block_shards(): pl.pallas_call(functools.partial(finish_kernel, own), out_shape=result, i...  5.76 us

profile of v3, /device:TPU:0, one launch (start us, length us, event | category | flops | bytes accessed | tf_op | source)
XLA Modules:
  0.0 137.7 jit_solution(12572661163488306303)
XLA Ops:
  0.7 131.1 %shard_map.316 = (bf16[2,1,256,384]{3,2,1,0:T(8,128)(2,1)}, bf16[2,1,256,384]{3,2,1,0:T(8,128)(2,1)}, bf16[12,2,2,32,768]{4,3,2,1,0:T(8,128)(2,1)}, bf16[12,2,2,...) custom-call(bf16[2,1,256,384]{3,2,1,0:T(8,128)(2,1)} %refs_0_.1, bf16[2,1,256,384]{3,2,1,0:T(8,128)(2,1)} %refs_1_.1, ...), custom_call_target="tpu_custom_call" | custom-call | tf_op jit(solution)/shard_map/pallas_call | solution.py:1264
  131.8 5.8 %shard_map.317 = (f32[1536,768]{1,0:T(8,128)}, f32[768,1536]{1,0:T(8,128)}, bf16[2,1,256,384]{3,2,1,0:T(8,128)(2,1)}, bf16[2,1,256,384]{3,2,1,0:T(8,128)(2,1)}, ...) custom-call(bf16[12,2,2,32,768]{4,3,2,1,0:T(8,128)(2,1)} %get-tuple-, ...), custom_call_target="tpu_custom_call" | custom-call | tf_op jit(solution)/shard_map/pallas_call | solution.py:1308

commit v4 on v3

--- a/solution.py
+++ b/solution.py
@@ -352,7 +352,7 @@
         return jnp.concatenate([column] * (pixels // column.shape[1]), axis=1)
 
     def partner(k):
-        return rank ^ lax.rem(7 * k, RANKS)
+        return rank ^ lax.rem(15 * k, RANKS)
 
     def slab_copy(sems, index, src, dst, d):
         return pltpu.make_async_remote_copy(
@@ -425,7 +425,6 @@
     v.rb1[rank] = v.tb[core, rank]
     for which in range(len(ASYNC)):
         bring(which).start()
-    loop(chunks, fetch)
     copy(v.tb.at[core], v.tb.at[core], v.tw, 0, twin).start()
     copy(v.vx.at[core], v.vx.at[core], v.tw, 1, twin).start()
 
@@ -527,16 +526,13 @@
     for l in range(RANKS):
         v.kh[l] = jnp.broadcast_to(taps[:, l : l + 1], (slab, 128))
 
-    pltpu.make_async_copy(v.wu, v.wu, v.fetch.at[0]).wait()
-    pltpu.make_async_copy(v.wd, v.wd, v.fetch.at[1]).wait()
-
     def turn(m):
         v.wut[m] = v.wu[m].T
         v.wdt[m] = v.wd[m].T
 
-    loop(chunks // 2, turn)
 
     all_slabs(v.a1, 1, v.rb1)
+    loop(chunks, fetch)
     step_rows = 4
 
     def convolve(b):
@@ -579,7 +575,9 @@
 
     copy(v.vx.at[core], v.vx.at[1 - core], v.tw, 1, twin).wait_recv()
     spread(1 - core, v.vx[1 - core])
-    loop(chunks, turn, chunks // 2)
+    pltpu.make_async_copy(v.wu, v.wu, v.fetch.at[0]).wait()
+    pltpu.make_async_copy(v.wd, v.wd, v.fetch.at[1]).wait()
+    loop(chunks, turn)
     v.branch[...] = jnp.zeros_like(v.branch)
     v.gn[...] = jnp.zeros_like(v.gn)
 
@@ -748,30 +746,34 @@
                 v.lags[l, at, cut] = total
 
         by_tiles(lag_rows)
-        none = jnp.zeros((slab, columns), F32)
-
-        def one_step(b, totals):
-            at = pl.ds(b * step_rows, step_rows)
-            shape = (step_rows, slab, columns)
-            values = v.galong[at].reshape(step_rows * slab, columns).astype(BF16)
-            g_both = by_table(values, v.to_hi, v.to_lo)
-            g_re, g_im = g_both[:, :columns].reshape(shape), g_both[:, columns:].reshape(shape)
-            x_re, x_im = v.xs[0, at], v.xs[1, at]
-            k0, k1, k2 = v.ks[0], v.ks[1], v.ks[2]
-            y_both = jnp.concatenate([g_re * k0 + g_im * k1, g_im * k2 - g_re * k1], axis=2)
-            y_both = y_both.reshape(step_rows * slab, 2 * columns)
-            conv = by_table(y_both, v.from_hi, v.from_lo)
-            v.sb4[at] = conv.reshape(shape).astype(BF16)
-            return (
-                totals[0] + (x_re * g_re).sum(axis=0),
-                totals[1] + (x_im * g_im).sum(axis=0),
-                totals[2] + (x_re * g_im - x_im * g_re).sum(axis=0),
-            )
-
-        cross = lax.fori_loop(0, RANKS // step_rows, one_step, (none, none, none))
-        v.rb4[rank] = v.sb4[rank]
-        for q in range(3):
-            v.cross[q] = cross[q]
+        v.cross[...] = jnp.zeros_like(v.cross)
+
+    def convolve_step(turn_of):
+        block = lax.rem(z + turn_of, RANKS // step_rows)
+        at = pl.ds(block * step_rows, step_rows)
+        shape = (step_rows, slab, columns)
+        values = v.galong[at].reshape(step_rows * slab, columns).astype(BF16)
+        g_both = by_table(values, v.to_hi, v.to_lo)
+        g_re, g_im = g_both[:, :columns].reshape(shape), g_both[:, columns:].reshape(shape)
+        x_re, x_im = v.xs[0, at], v.xs[1, at]
+        k0, k1, k2 = v.ks[0], v.ks[1], v.ks[2]
+        y_both = jnp.concatenate([g_re * k0 + g_im * k1, g_im * k2 - g_re * k1], axis=2)
+        y_both = y_both.reshape(step_rows * slab, 2 * columns)
+        conv = by_table(y_both, v.from_hi, v.from_lo)
+        v.sb4[at] = conv.reshape(shape).astype(BF16)
+        v.cross[0] += (x_re * g_re).sum(axis=0)
+        v.cross[1] += (x_im * g_im).sum(axis=0)
+        v.cross[2] += (x_re * g_im - x_im * g_re).sum(axis=0)
+        for q in range(step_rows):
+            d = block * step_rows + q
+
+            @pl.when(d != rank)
+            def _():
+                slab_copy(v.a4, 0, v.sb4.at[d], v.rb4.at[rank], d).start()
+
+            @pl.when(d == rank)
+            def _():
+                v.rb4[rank] = v.sb4[rank]
 
     def kernel_grads():
         cross = [v.cross[q] for q in range(3)]
@@ -793,7 +795,6 @@
         for q in range(lanes // 128):
             cut = slice(q * 128, (q + 1) * 128)
             v.kth[:, cut] = jnp.sum(lags * v.pick[:, cut][None], axis=1)
-        parameters()
 
     def parameters():
         def moments(dk, e_re, e_im):
@@ -834,15 +835,17 @@
         ]
         table = jnp.concatenate(rows, axis=0)
         z, y, x = rank // 4, (rank // 2) % 2, rank % 2
+        blocks = [jnp.zeros((per, 128), F32) for _ in range(3)]
+        at = lax.broadcasted_iota(jnp.int32, (128, lanes), 0)
+        at -= lax.broadcasted_iota(jnp.int32, (128, lanes), 1) // per
+        for k in range(5):
+            chosen = (at == k * own).astype(BF16)
+            for five in range(3 if k < 4 else 2):
+                r = 5 * five + k
+                values = (v.of_mode[...] * table[r : r + 1]).astype(BF16)
+                blocks[five] += lax.dot_general(values, chosen, NT, preferred_element_type=F32)
         for five in range(3):
-            block = jnp.zeros((per, 128), F32)
-            for k in range(5 if five < 2 else 4):
-                r = 5 * five + k
-                at = lax.broadcasted_iota(jnp.int32, (128, lanes), 0) - k * own
-                at = (at == lax.broadcasted_iota(jnp.int32, (128, lanes), 1) // per).astype(BF16)
-                values = (v.of_mode[...] * table[r : r + 1]).astype(BF16)
-                block += lax.dot_general(values, at, NT, preferred_element_type=F32)
-            v.pack[five * per : (five + 1) * per, :] = block.astype(BF16)
+            v.pack[five * per : (five + 1) * per, :] = blocks[five].astype(BF16)
         ones = jnp.ones((8, 128), F32)
         vectors = [
             v.dbu[m, 0:1, q * 128 : (q + 1) * 128] for m in range(chunks) for q in range(part // 128)
@@ -877,6 +880,11 @@
         mine = v.gathered.at[:, :, x]
         copy(mine, mine, v.ga, 5, beside).start()
 
+    def gather_done():
+        theirs = v.gathered.at[:, :, 1 - x]
+        copy(theirs, theirs, v.ga, 5, beside).wait_recv()
+        pltpu.make_async_copy(v.gathered, v.all_gathered, v.leave.at[4]).start()
+
     def token_grads():
         all_slabs(v.a4, 1, v.rb4)
 
@@ -937,49 +945,56 @@
 
     events = {
         0: norm_back,
-        3: outputs,
-        9: convolve_back,
-        11: kernel_grads,
-        13: gather_across,
-        15: gather_beside,
-        21: token_grads,
+        1: outputs,
+        3: convolve_back,
+        7: kernel_grads,
+        8: parameters,
+        10: gather_across,
+        12: gather_beside,
+        20: gather_done,
+        16: token_grads,
     }
 
     def feed_and_send(t):
         feed(t)
         for q in range(CUTS):
             c = CUTS * t + q
-            advance(0, c, (c < 4).astype(jnp.int32) * (1 + middle))
+            advance(0, c, (c < 6).astype(jnp.int32) * (1 + middle))
+        known(1, t - 3)
+        known(2, t - 3 - 2)
 
     loop(chunks, feed_and_send)
     share()
+    for ahead in range(chunks - 3, 4):
+        known(1, jnp.int32(ahead))
+        known(2, jnp.int32(ahead - 2))
+        known(3, jnp.int32(ahead - 4))
 
     def tick(t, carry):
         for when, event in events.items():
             pl.when(t == when)(event)
-        for when, sems, src, dst in (
-            (0, v.a3, v.sb3, v.rb3),
-            (9, v.a4, v.sb4, v.rb4),
-        ):
-            batch = t - when
-
-            @pl.when(batch * (8 - 1 - batch) >= 0)
-            def _():
-                scatter(sems, src, dst.at[rank], first=1 + 2 * batch, count=2)
+        batch = t - 0
+
+        @pl.when(batch * (2 - 1 - batch) >= 0)
+        def _():
+            scatter(v.a3, v.sb3, v.rb3.at[rank], first=1 + 8 * batch, count=8)
+
+        turn_of = t - 3
+
+        @pl.when(turn_of * (RANKS // step_rows - 1 - turn_of) >= 0)
+        def _():
+            convolve_step(turn_of)
 
         for q in range(1):
-            c = 4 + 1 * (t - 0) + q
+            c = 6 + 1 * (t - 0) + q
             known(0, jnp.where(t < 0, pieces, c))
         for stage, start in enumerate((0,2,4,6,8,10,12,14,16), 1):
-            for q in range(1):
-                known(stage, 1 * (t - start) + q)
+            known(stage, t + 4 - start)
         return carry
 
-    lax.fori_loop(0, pieces // 1 + (0,2,4,6,8,10,12,14,16)[-1], tick, 0)
-
-    theirs = v.gathered.at[:, :, 1 - x]
-    copy(theirs, theirs, v.ga, 5, beside).wait_recv()
-
+    lax.fori_loop(0, pieces + (0,2,4,6,8,10,12,14,16)[-1] - 4, tick, 0)
+
+    pltpu.make_async_copy(v.gathered, v.all_gathered, v.leave.at[4]).wait()
     pltpu.make_async_copy(v.fd, v.down, v.leave.at[0]).wait()
     pltpu.make_async_copy(v.fu, v.up, v.leave.at[1]).wait()
     pltpu.make_async_copy(v.o_out, v.output, v.leave.at[2]).wait()
@@ -1169,7 +1184,10 @@
         d_tokens=(jax.ShapeDtypeStruct(tokens.shape, BF16), anywhere),
         down=(jax.ShapeDtypeStruct(down_shape, BF16), anywhere),
         up=(jax.ShapeDtypeStruct(up_shape, BF16), anywhere),
-        gathered=(jax.ShapeDtypeStruct((4, 2, 2, 3 * modes_each + 32, 128), BF16), in_vmem),
+        all_gathered=(
+            jax.ShapeDtypeStruct((4, 2, 2, 3 * modes_each + 32, 128), BF16),
+            anywhere,
+        ),
     )
     low_slabs = pltpu.VMEM(slabs, BF16)
     both_slabs = pltpu.VMEM((2,) + slabs, BF16)
@@ -1224,7 +1242,8 @@
         sums=pltpu.VMEM((5, here, 128), F32),
         pack=pltpu.VMEM((3 * modes_each + 32, 128), BF16),
         fetch=pltpu.SemaphoreType.DMA((2,)),
-        leave=pltpu.SemaphoreType.DMA((4,)),
+        leave=pltpu.SemaphoreType.DMA((5,)),
+        gathered=pltpu.VMEM((4, 2, 2, 3 * modes_each + 32, 128), BF16),
         bring=pltpu.SemaphoreType.DMA((len(ASYNC),)),
         o_out=pltpu.VMEM(tokens.shape, BF16),
         t_out=pltpu.VMEM(tokens.shape, BF16),

time: 138 us -> 133 us (0.964)
  Pallas kernels: 137 us -> 132 us
    pallas_call x1, Pallas kernels: 131 us -> 127 us  [block_shards(): pl.pallas_call(functools.partial(block_kernel, names), out_shape=tuple((s...]
where the time goes in v4:
time: 133 us
  Pallas kernels  132 us (99%)
    pallas_call x1, Pallas kernels, block_shards(): pl.pallas_call(functools.partial(block_kernel, names), out_shape=tuple((s...  127 us
    pallas_call x1, Pallas kernels, block_shards(): pl.pallas_call(functools.partial(finish_kernel, own), out_shape=result, i...  5.76 us

profile of v4, /device:TPU:0, one launch (start us, length us, event | category | flops | bytes accessed | tf_op | source)
XLA Modules:
  0.0 133.2 jit_solution(13827625674237587973)
XLA Ops:
  0.7 126.6 %shard_map.316 = (bf16[2,1,256,384]{3,2,1,0:T(8,128)(2,1)}, bf16[2,1,256,384]{3,2,1,0:T(8,128)(2,1)}, bf16[12,2,2,32,768]{4,3,2,1,0:T(8,128)(2,1)}, bf16[12,2,2,...) custom-call(bf16[2,1,256,384]{3,2,1,0:T(8,128)(2,1)} %refs_0_.1, bf16[2,1,256,384]{3,2,1,0:T(8,128)(2,1)} %refs_1_.1, ...), custom_call_target="tpu_custom_call" | custom-call | tf_op jit(solution)/shard_map/pallas_call | solution.py:1283
  127.3 5.8 %shard_map.317 = (f32[1536,768]{1,0:T(8,128)}, f32[768,1536]{1,0:T(8,128)}, bf16[2,1,256,384]{3,2,1,0:T(8,128)(2,1)}, bf16[2,1,256,384]{3,2,1,0:T(8,128)(2,1)}, ...) custom-call(bf16[12,2,2,32,768]{4,3,2,1,0:T(8,128)(2,1)} %get-tuple-, ...), custom_call_target="tpu_custom_call" | custom-call | tf_op jit(solution)/shard_map/pallas_call | solution.py:1327

commit v5 on v4

--- a/solution.py
+++ b/solution.py
@@ -74,6 +74,7 @@
 
 RANKS = 16
 STAGES = 10
+SLOTS = (0, 2, 3, 2, 3, 4, 5, 4, 1)
 CUTS = 2
 ASYNC = (
     ("cotangent_in", "cotangent"),
@@ -142,13 +143,13 @@
             src_ref=src,
             dst_ref=dst,
             send_sem=send.at[kind],
-            recv_sem=recv.at[kind, c],
+            recv_sem=recv.at[SLOTS[kind], c],
             device_id=target,
             device_id_type=MESH,
         ).start()
 
     def landed(kind, ref):
-        pltpu.make_async_copy(ref, ref, recv.at[kind, c]).wait()
+        pltpu.make_async_copy(ref, ref, recv.at[SLOTS[kind], c]).wait()
 
     halves = lines[0].part.at[c]
     quarters = lines[0].from_first.at[c]
@@ -164,9 +165,9 @@
             place = line.full.at[c, line.keep, which]
             start(kind, place, place, target)
 
-    def give_back():
+    def give_back(which):
         for line in lines:
-            place = line.full.at[c, line.keep]
+            place = line.full.at[c, line.keep, which]
             start(8, place, place, line.first)
 
     if stage == 0:
@@ -228,6 +229,7 @@
                 mine = line.part.at[c, line.keep, near]
                 line.full[c, line.keep, near] = added(mine, line.from_third.at[c])
             give(5, near, inner)
+            give_back(near)
 
     elif stage == 6:
 
@@ -235,6 +237,7 @@
         def _():
             landed(5, quarters)
             give(6, near, inner)
+            give_back(near)
 
     elif stage == 7:
 
@@ -242,14 +245,14 @@
         def _():
             landed(6, quarters)
             give(7, far, outer)
-            give_back()
+            give_back(far)
 
     elif stage == 8:
 
         @pl.when(role == 1)
         def _():
             landed(7, quarters)
-            give_back()
+            give_back(far)
 
     else:
 
@@ -1277,7 +1280,7 @@
     scratch.update(a1=one_each, a3=one_each, a4=one_each, fw=one_each)
     scratch.update(a2=pltpu.SemaphoreType.DMA((2, RANKS)))
     scratch.update(sent=pltpu.SemaphoreType.DMA((9,)))
-    scratch.update(landed=pltpu.SemaphoreType.DMA((9, CUTS * chunks)))
+    scratch.update(landed=pltpu.SemaphoreType.DMA((6, CUTS * chunks)))
     scratch.update(tw=pltpu.SemaphoreType.DMA((2, 5)), ga=pltpu.SemaphoreType.DMA((2, 6)))
     names = tuple(inputs) + tuple(outs) + tuple(scratch)
     output, d_tokens, down, up, gathered = pl.pallas_call(

time: 133 us -> 131 us (0.985)
  Pallas kernels: 132 us -> 130 us
    pallas_call x1, Pallas kernels: 127 us -> 124 us  [block_shards(): pl.pallas_call(functools.partial(block_kernel, names), out_shape=tuple((s...]
where the time goes in v5:
time: 131 us
  Pallas kernels  130 us (99%)
    pallas_call x1, Pallas kernels, block_shards(): pl.pallas_call(functools.partial(block_kernel, names), out_shape=tuple((s...  124 us
    pallas_call x1, Pallas kernels, block_shards(): pl.pallas_call(functools.partial(finish_kernel, own), out_shape=result, i...  5.76 us

profile of v5, /device:TPU:0, one launch (start us, length us, event | category | flops | bytes accessed | tf_op | source)
XLA Modules:
  0.0 130.7 jit_solution(3364811310832146439)
XLA Ops:
  0.7 124.1 %shard_map.316 = (bf16[2,1,256,384]{3,2,1,0:T(8,128)(2,1)}, bf16[2,1,256,384]{3,2,1,0:T(8,128)(2,1)}, bf16[12,2,2,32,768]{4,3,2,1,0:T(8,128)(2,1)}, bf16[12,2,2,...) custom-call(bf16[2,1,256,384]{3,2,1,0:T(8,128)(2,1)} %refs_0_.1, bf16[2,1,256,384]{3,2,1,0:T(8,128)(2,1)} %refs_1_.1, ...), custom_call_target="tpu_custom_call" | custom-call | tf_op jit(solution)/shard_map/pallas_call | solution.py:1286
  124.7 5.8 %shard_map.317 = (f32[1536,768]{1,0:T(8,128)}, f32[768,1536]{1,0:T(8,128)}, bf16[2,1,256,384]{3,2,1,0:T(8,128)(2,1)}, bf16[2,1,256,384]{3,2,1,0:T(8,128)(2,1)}, ...) custom-call(bf16[12,2,2,32,768]{4,3,2,1,0:T(8,128)(2,1)} %get-tuple-, ...), custom_call_target="tpu_custom_call" | custom-call | tf_op jit(solution)/shard_map/pallas_call | solution.py:1330

commit v6 on v5

--- a/solution.py
+++ b/solution.py
@@ -581,7 +581,6 @@
     pltpu.make_async_copy(v.wu, v.wu, v.fetch.at[0]).wait()
     pltpu.make_async_copy(v.wd, v.wd, v.fetch.at[1]).wait()
     loop(chunks, turn)
-    v.branch[...] = jnp.zeros_like(v.branch)
     v.gn[...] = jnp.zeros_like(v.gn)
 
     def forward(k):
@@ -655,13 +654,23 @@
         for q in range(CUTS):
             v.pu[CUTS * t + q] = up[up_cut(up.shape, q)].reshape(v.pu.shape[1:])
         v.gn[...] += jnp.dot(v.wu[t], g_hidden, preferred_element_type=F32)
-        v.branch[...] += jnp.dot(v.wdt[t], active, preferred_element_type=F32)
+        v.active[t] = active
         ones = jnp.ones((8, pixels), BF16)
         v.dbu[t] = lax.dot_general(ones, g_hidden, NT, preferred_element_type=F32)
 
     def share():
         v.gn_out[...] = v.gn[...].astype(BF16)
         copy(v.gn_out, v.gn_in, v.tw, 3, twin).start()
+
+    def branches():
+        def rows(q):
+            at = pl.ds(pl.multiple_of(q * 128, 128), 128)
+            total = jnp.dot(v.wdt[0, at, :], v.active[0], preferred_element_type=F32)
+            for m in range(1, chunks):
+                total += jnp.dot(v.wdt[m, at, :], v.active[m], preferred_element_type=F32)
+            v.branch[at, :] = total
+
+        loop(channels // 128, rows)
         theirs = pl.ds(pl.multiple_of((1 - core) * here, here), here)
         v.br_out[...] = v.branch[theirs, :].astype(BF16)
         copy(v.br_out, v.br_in, v.tw, 4, twin).start()
@@ -948,13 +957,14 @@
 
     events = {
         0: norm_back,
-        1: outputs,
+        1: branches,
+        6: outputs,
         3: convolve_back,
-        7: kernel_grads,
-        8: parameters,
-        10: gather_across,
-        12: gather_beside,
-        20: gather_done,
+        8: kernel_grads,
+        9: parameters,
+        12: gather_across,
+        14: gather_beside,
+        21: gather_done,
         16: token_grads,
     }
 
@@ -1236,6 +1246,7 @@
         xhat=pltpu.VMEM((2 * RANKS, own, pixels), F32),
         normed=pltpu.VMEM((channels, pixels), BF16),
         branch=pltpu.VMEM((channels, pixels), F32),
+        active=pltpu.VMEM((chunks, part, pixels), BF16),
         gn=pltpu.VMEM((channels, pixels), F32),
         gn_out=pltpu.VMEM((channels, pixels), BF16),
         gn_in=pltpu.VMEM((channels, pixels), BF16),

time: 131 us -> 130 us (level)
  no operation moved by 1% of the time
where the time goes in v6:
time: 130 us; the launch traced here: 129 us
  Pallas kernels  129 us (99%)
    pallas_call x1, Pallas kernels, block_shards(): pl.pallas_call(functools.partial(block_kernel, names), out_shape=tuple((s...  123 us
    pallas_call x1, Pallas kernels, block_shards(): pl.pallas_call(functools.partial(finish_kernel, own), out_shape=result, i...  5.76 us

profile of v6, /device:TPU:0, one launch (start us, length us, event | category | flops | bytes accessed | tf_op | source)
XLA Modules:
  0.0 129.4 jit_solution(11448822479129414704)
XLA Ops:
  0.7 122.8 %shard_map.316 = (bf16[2,1,256,384]{3,2,1,0:T(8,128)(2,1)}, bf16[2,1,256,384]{3,2,1,0:T(8,128)(2,1)}, bf16[12,2,2,32,768]{4,3,2,1,0:T(8,128)(2,1)}, bf16[12,2,2,...) custom-call(bf16[2,1,256,384]{3,2,1,0:T(8,128)(2,1)} %refs_0_.1, bf16[2,1,256,384]{3,2,1,0:T(8,128)(2,1)} %refs_1_.1, ...), custom_call_target="tpu_custom_call" | custom-call | tf_op jit(solution)/shard_map/pallas_call | solution.py:1297
  123.4 5.8 %shard_map.317 = (f32[1536,768]{1,0:T(8,128)}, f32[768,1536]{1,0:T(8,128)}, bf16[2,1,256,384]{3,2,1,0:T(8,128)(2,1)}, bf16[2,1,256,384]{3,2,1,0:T(8,128)(2,1)}, ...) custom-call(bf16[12,2,2,32,768]{4,3,2,1,0:T(8,128)(2,1)} %get-tuple-, ...), custom_call_target="tpu_custom_call" | custom-call | tf_op jit(solution)/shard_map/pallas_call | solution.py:1341
